TPU v7x, 256 devices: a whole 4x4x8 slice. The times are simulated.
256 devices in a mesh: member: 16 (over y, x), region: 16 (over z, core).
Axes of the slice: x: 4, y: 4, z: 8, core: 2. Of those that a mesh axis runs over, the one named last changes fastest.
Arguments:
- states: float32 [256, 393216], P('member', 'region'), may hold values from -6 to 6
- weights: float32 [256, 393216], P('member', 'region'), may hold values from -6 to 6
- obs_count: int32 [3072], P('region'), may hold values from 0 to 32
- neighbours: int32 [3072, 12], P('region'), may hold values from 0 to 3071, as said below
Outputs:
- increments: float32 [256, 393216], P('member', 'region')
Inputs may be any that keep to these rules, and one draw needn't show every extreme that they name: `neighbours`: each row lists 12 distinct tiles, all within 8 tiles of its own tile counting cyclically over the 3072 tiles; the list always holds the tile itself and the tiles exactly 8 before and after it, in a drawn order.
All inputs are finite; a program needn't handle non-finite values.
Results may differ from a plain program's by a relative error of at most 0.0003.
Values sent between devices are 32-bit elements; how exact they have to be, the bound alone decides.
No kernel may reach another device: no remote copies, remote signals or barrier semaphores. Data moves between devices by JAX's collectives and lax.ppermute only.
A program may use at most 128 MiB of HBM per device.

v0:
```python
import jax
import jax.numpy as jnp
from jax import lax
from jax.sharding import PartitionSpec as P

TILE = 128
HALO_TILES = 8
TPD = 12


def extended_2(block, sides, width):
    for axis, dim in sides:
        count = lax.axis_size(axis)
        forward = [(i, i + 1) for i in range(count - 1)]
        forward.append((count - 1, 0))
        backward = [(target, source) for source, target in forward]
        low = lax.ppermute(
            lax.slice_in_dim(block, block.shape[dim] - width, None, axis=dim), axis, forward
        )
        high = lax.ppermute(lax.slice_in_dim(block, 0, width, axis=dim), axis, backward)
        block = jnp.concatenate([low, block, high], axis=dim)
    return block


def taper(offset, tile):
    rows = jnp.arange(tile, dtype=jnp.float32)
    spread = tile * offset[:, None, None] + rows[None, None, :] - rows[None, :, None]
    scaled = spread / (2.0 * tile)
    return 1.0 / (1.0 + scaled * scaled)


def shards(states, weights, obs_count, neighbours):
    member_count = lax.axis_size("member")
    region_count = lax.axis_size("region")
    member_part, local_rows = states.shape
    local_tiles = local_rows // TILE
    counts = obs_count.astype(jnp.float32)
    factor = counts / (counts + 8.0)
    scaled = (weights.reshape(member_part, local_tiles, TILE) * factor[None, :, None]).reshape(
        member_part, local_rows
    )
    stacked = jnp.stack([states, scaled])
    rim = HALO_TILES * TILE
    block = TPD * TILE
    padded = extended_2(stacked, (("region", 2),), rim)
    own_block = lax.all_to_all(stacked, "member", split_axis=2, concat_axis=1, tiled=True)
    extended = extended_2(own_block, (("member", 2),), rim)
    below, above = (
        lax.all_gather(padded[:, :, :rim], "member", axis=1, tiled=True),
        lax.all_gather(padded[:, :, rim + local_rows :], "member", axis=1, tiled=True),
    )
    position = lax.axis_index("member")
    lower = jnp.where(position == 0, below, extended[:, :, :rim])
    upper = jnp.where(position == member_count - 1, above, extended[:, :, rim + block :])
    window = jnp.concatenate([lower, extended[:, :, rim : rim + block], upper], axis=2)
    members = window.shape[1]
    anomaly = window[0] - jnp.mean(window[0], axis=0, keepdims=True)
    window_weights = window[1]
    tiles_all = TPD * member_count * region_count
    first_tile = (lax.axis_index("region") * member_count + lax.axis_index("member")) * TPD
    lists = lax.dynamic_slice_in_dim(neighbours, lax.axis_index("member") * TPD, TPD, 0)
    local_ids = (lists - first_tile + HALO_TILES) % tiles_all
    span_count = 2 * HALO_TILES + 1
    tile_places = jnp.arange(TPD, dtype=jnp.int32)
    shift_places = jnp.arange(span_count, dtype=jnp.int32)
    wanted = tile_places[:, None, None] + shift_places[None, None, :]
    keep_table = jnp.sum((local_ids[:, :, None] == wanted).astype(jnp.float32), axis=1)
    mine = anomaly[:, rim : rim + block].reshape(members, TPD, TILE)

    def add_offset(shift, total):
        others = lax.dynamic_slice_in_dim(anomaly, shift * TILE, block, 1).reshape(
            members, TPD, TILE
        )
        other_weights = lax.dynamic_slice_in_dim(window_weights, shift * TILE, block, 1).reshape(
            members, TPD, TILE
        )
        covar = jnp.einsum("mti,mtj->tij", mine, others, precision=lax.Precision.HIGHEST) / (
            members - 1.0
        )
        offset = jnp.full((TPD,), shift - HALO_TILES).astype(jnp.float32)
        keep = lax.dynamic_index_in_dim(keep_table, shift, 1, keepdims=False)
        coefficient = taper(offset, TILE) * covar * keep[:, None, None]
        return total + jnp.einsum(
            "mtj,tij->mti", other_weights, coefficient, precision=lax.Precision.HIGHEST
        )

    total = lax.fori_loop(0, span_count, add_offset, jnp.zeros((members, TPD, TILE), jnp.float32))
    returned = lax.all_to_all(
        total.reshape(members, block), "member", split_axis=0, concat_axis=1, tiled=True
    )
    return returned


def solution(mesh):
    placed = (P("member", "region"), P("member", "region"), P("region"), P("region", None))
    return jax.shard_map(
        shards, mesh=mesh, in_specs=placed, out_specs=P("member", "region"), check_vma=False
    )
```

profile of v0, /device:TPU:96, one launch (start us, length us, event | category | flops | bytes accessed | tf_op | source)
XLA Modules:
  0.0 547.6 jit_solution(15014115736776766271)
XLA Ops:
  16.0 27.3 %copy.49 = f32[2,16,24576]{1,0,2:T(2,128)} copy(f32[2,16,24576]{2,1,0:T(8,128)} %pad_maximum_fusion.1) | data formatting | bytes 6291456 | tf_op jit(solution)/shard_map/stack | solution.py:42
  43.4 36.6 %reshape.73 = f32[16,1,49152]{2,1,0:T(1,128)} reshape(f32[24576,2,16]{2,1,0:T(2,128)} %bitcast.55) | data formatting | bytes 6291456
  79.9 7.0 %all-to-all-start = ((f32[16,1,49152]{2,1,0:T(1,128)}), f32[16,1,49152]{2,1,0:T(1,128)S(1)}, u32[]{:S(2)}, u32[]{:S(2)}) async-start(f32[16,1,49152]{2,1,0:T(1,128)} %reshape.73), calls=%async_computation | async-start | bytes 6291456 | tf_op jit(solution)/shard_map/all_to_all | solution.py:46
  90.2 47.7 %all-to-all-done = f32[16,1,49152]{2,1,0:T(1,128)S(1)} async-done(((f32[16,1,49152]{2,1,0:T(1,128)}), f32[16,1,49152]{2,1,0:T(1,128)S(1)}, u32[]{:S(2)}, u32[]{:S(2)}) %all-to-all-start) | async-done | bytes 3145760 | tf_op jit(solution)/shard_map/all_to_all | solution.py:46
  140.1 10.1 %reduce.1 = f32[16,49152]{1,0:T(8,128)S(1)} reduce(f32[16,1,49152]{2,1,0:T(1,128)} %copy-done.1, f32[]{:T(128)} %broadcast.103), dimensions={1}, to_apply=%all_to_all.27.reduce_sub_computation | reduce | bytes 6291460 | tf_op jit(solution)/shard_map/all_to_all | solution.py:46
  150.2 43.7 %reshape.74 = f32[24576,2,16]{2,1,0:T(2,128)} reshape(f32[16,49152]{1,0:T(8,128)S(1)} %reduce.1) | data formatting | bytes 6291456
  193.9 30.1 %copy.63 = f32[2,16,16,1536]{3,1,2,0:T(8,128)S(1)} copy(f32[2,16,16,1536]{1,0,3,2:T(2,128)} %bitcast.56) | data formatting | bytes 6291456 | tf_op jit(solution)/shard_map/all_to_all | solution.py:46
  226.5 5.3 collective-permute-start.3
  232.2 45.1 %collective-permute-done.1 = f32[2,256,1024]{2,1,0:T(8,128)} collective-permute-done((f32[2,256,1024]{2,1,0:T(8,128)}, f32[2,256,1024]{2,1,0:T(8,128)}, u32[]{:S(2)}, u32[]{:S(2)}) %collective-permute-start.1) | collective-permute-done | bytes 2097184 | tf_op jit(solution)/shard_map/ppermute | solution.py:17
  290.4 219.8 %while.16 = (s32[]{:T(128)}, f32[256,12,128]{0,2,1:T(8,128)}, f32[256,3584]{1,0:T(8,128)}, f32[256,12,128]{2,0,1:T(8,128)}, f32[12,17]{0,1:T(8,128)S(1)}, /*inde...) while((s32[]{:T(128)}, f32[256,12,128]{0,2,1:T(8,128)}, ...), condition=%wide.region_3.4_spmd.clone, body=%wide.region_2.3_spmd.clone.sunk | while | flops 1210318976 | bytes 22021480 | solution.py:87
  294.1 4.4 fusion.22
  306.6 4.4 fusion.22
  319.5 4.4 fusion.22
  332.5 4.4 fusion.22
  345.5 4.4 fusion.22
  358.4 4.4 fusion.22
  371.4 4.4 fusion.22
  384.3 4.4 fusion.22
  397.3 4.4 fusion.22
  410.3 4.4 fusion.22
  436.2 4.4 fusion.22
  462.1 4.4 fusion.22
  488.0 4.4 fusion.22
  513.7 25.8 %all_to_all.37 = f32[16,16,1536]{2,1,0:T(8,128)S(1)} all-to-all(f32[16,16,1536]{2,1,0:T(8,128)} %all_to_all.31), channel_id=1, replica_groups=mesh['member'=16,'region'=16] {'member'}, dimensions={0} | all-to-all | bytes 3145728 | tf_op jit(solution)/shard_map/all_to_all | solution.py:88
  (157 shorter events, 197.4 us)
Async XLA Ops:
  6.5 2.5 copy-start.3
  6.5 225.7 %all-gather.3.cloned.1.call-start = ((), (), s32[]{:S(2)}) async-start(), calls=%async_computation.2 | async-start | bytes 2228224 | tf_op jit(solution)/shard_map/all_gather | solution.py:49
  9.0 4.4 collective-permute-start
  13.5 0.6 copy-start.4
  79.9 58.0 %all-to-all-start = ((f32[16,1,49152]{2,1,0:T(1,128)}), f32[16,1,49152]{2,1,0:T(1,128)S(1)}, u32[]{:S(2)}, u32[]{:S(2)}) async-start(f32[16,1,49152]{2,1,0:T(1,128)} %reshape.73), calls=%async_computation | async-start | bytes 6291456 | tf_op jit(solution)/shard_map/all_to_all | solution.py:46
  87.0 193.8 %all-gather.5.cloned.1.call-start = ((), (), s32[]{:S(2)}) async-start(), calls=%async_computation.3 | async-start | bytes 2228224 | tf_op jit(solution)/shard_map/all_gather | solution.py:50
  87.0 2.5 collective-permute-start.2
  89.6 0.6 copy-start.5
  137.9 1.6 copy-start.1
  224.0 7.8 %copy-start.6 = (s32[192,12]{0,1:T(8,128)S(1)}, s32[192,12]{0,1:T(8,128)}, u32[]{:S(2)}) copy-start(s32[192,12]{0,1:T(8,128)} %param.9) | copy-start | bytes 27652
  226.5 50.8 %collective-permute-start.1 = (f32[2,256,1024]{2,1,0:T(8,128)}, f32[2,256,1024]{2,1,0:T(8,128)}, u32[]{:S(2)}, u32[]{:S(2)}) collective-permute-start(f32[2,256,1024]{2,1,0:T(8,128)} %get-tuple-element.227), channel_id=1, source_target_pairs={{0,16},{16,32},{32,48},{48,64},{64,80},{80,96},{96,112},{112,128},... | collective-permute-start | bytes 6291464 | tf_op jit(solution)/shard_map/ppermute | solution.py:17
  226.5 54.3 %collective-permute-start.3 = (f32[2,256,1024]{2,1,0:T(8,128)}, f32[2,256,1024]{2,1,0:T(8,128)}, u32[]{:S(2)}, u32[]{:S(2)}) collective-permute-start(f32[2,256,1024]{2,1,0:T(8,128)} %get-tuple-element.228), channel_id=1, source_target_pairs={{16,0},{32,16},{48,32},{64,48},{80,64},{96,80},{112,96},{128,112},... | collective-permute-start | bytes 6291464 | tf_op jit(solution)/shard_map/ppermute | solution.py:20
  280.8 2.2 copy-start.2
  286.2 1.8 copy-start
Sparse Core Ops, SparseCore 0:
  14.2 53.0 all-gather.2
  90.4 69.1 all-gather.4
where the time goes:
time: 551 us; the launch traced here: 548 us
  local copies, waits for them, and re-layouts  224 us (41%)
  matrix products  148 us (27%)
  waiting for transfers between devices  99.7 us (18%)
  blocking collectives  25.8 us (5%)
  other arithmetic  23.6 us (4%)
  between operations  13.5 us (2%)
  starting transfers between devices  12.5 us (2%)
    unnamed x18, local copies, waits for them, and re-layouts  86.9 us
    dot_general x17, matrix products, add_offset(): jnp.einsum('mti,mtj->tij', mine, others, precision=lax.Precision.HIGHEST)  75.4 us
    dot_general x17, matrix products, add_offset(): jnp.einsum('mtj,tij->mti', other_weights, coefficient, precision=lax.Prec...  72.7 us
    ppermute x2, waiting for transfers between devices, extended_2(): lax.ppermute(lax.slice_in_dim(block, block.shape[dim] - width, None, axis...  49.5 us
    all_to_all x1, waiting for transfers between devices, shards(): lax.all_to_all(stacked, 'member', split_axis=2, concat_axis=1, tiled=True)  47.7 us
    dynamic_slice x34, local copies, waits for them, and re-layouts, add_offset(): lax.dynamic_slice_in_dim(window_weights, shift * TILE, block, 1)  43.3 us
    all_to_all x2, local copies, waits for them, and re-layouts, shards(): lax.all_to_all(stacked, 'member', split_axis=2, concat_axis=1, tiled=True)  30.6 us
    dynamic_slice x17, local copies, waits for them, and re-layouts, add_offset(): lax.dynamic_slice_in_dim(anomaly, shift * TILE, block, 1)  27.9 us
  transfers between devices with their start and end apart: 7, of which 4 were waited for; matrix products, arithmetic and copies ran while one was open for 29% of the time, Pallas kernels for 0%

commit v1 on v0

v1 whole, which is shorter than its diff:
```python
import jax
import jax.numpy as jnp
from jax import lax
from jax.experimental import pallas as pl
from jax.experimental.pallas import tpu as pltpu
from jax.sharding import PartitionSpec as P

TILE = 128
HALO = 8
OWN = 12
CHIP = 2 * OWN
PART = (CHIP + 2 * HALO) // 2
WINDOW = OWN + 2 * HALO
PAIRS = OWN // 2
SPAN = 2 * HALO + 2
BF = jnp.bfloat16
F32 = jnp.float32


def split(x):
    high = x.astype(BF)
    return high, (x - high.astype(F32)).astype(BF)


def dot(a, b):
    return jnp.dot(a, b, preferred_element_type=F32)


def enkf_kernel(core_ref, mask_ref, mine_ref, other_ref, out_ref, ath, atl, ah, al, wh, wl, taper, ch, cl):
    core = core_ref[0]
    members = out_ref.shape[0]

    def place(ref, t, w):
        lanes = pl.ds(pl.multiple_of(t * TILE, TILE), TILE)
        there = pl.ds(pl.multiple_of(w * TILE, TILE), TILE)
        state = ref[:, 0, :, lanes].reshape(members, TILE)
        anomaly = state - jnp.sum(state, axis=0, keepdims=True) * (1.0 / members)
        ah[:, there], al[:, there] = split(anomaly)
        ath[there, :], atl[there, :] = split(anomaly.T)
        wh[:, there], wl[:, there] = split(ref[:, 1, :, lanes].reshape(members, TILE))

    @pl.loop(0, PART)
    def _(t):
        first = t < OWN
        w = jnp.where(core == 0, t, jnp.where(first, t + 16, t - 4))
        place(mine_ref, t, w)

    @pl.loop(0, HALO)
    def _(t):
        place(other_ref, t, t + 20 * (1 - core))

    @pl.loop(0, SPAN)
    def _(k):
        rows = lax.broadcasted_iota(jnp.int32, (TILE, 2 * TILE), 0)
        columns = lax.broadcasted_iota(jnp.int32, (TILE, 2 * TILE), 1)
        scaled = (rows - columns + (k - HALO) * TILE).astype(F32) / (2.0 * TILE)
        taper[pl.ds(pl.multiple_of(k * TILE, TILE), TILE), :] = 1.0 / (1.0 + scaled * scaled)

    @pl.loop(0, PAIRS)
    def _(pair):
        first = pl.multiple_of(pair * 2 * TILE, 2 * TILE)
        band = pl.ds(first, SPAN * TILE)
        own = pl.ds(pl.multiple_of(first + HALO * TILE, 2 * TILE), 2 * TILE)
        own_high, own_low = ah[:, own], al[:, own]
        for k in range(0, SPAN, 2):
            rows = pl.ds(pl.multiple_of(first + k * TILE, 2 * TILE), 2 * TILE)
            high = ath[rows, :]
            covar = dot(high, own_high) + (dot(atl[rows, :], own_high) + dot(high, own_low))
            covar = covar * taper[k * TILE : (k + 2) * TILE, :]
            for half in range(2):
                keep = mask_ref[pl.ds(pair * SPAN + k + half, 1), :]
                coefficient = covar[half * TILE : (half + 1) * TILE] * keep
                spot = slice((k + half) * TILE, (k + half + 1) * TILE)
                ch[spot, :], cl[spot, :] = split(coefficient)
        out_ref[:, pl.ds(first, 2 * TILE)] = dot(wh[:, band], ch[...]) + (
            dot(wl[:, band], ch[...]) + dot(wh[:, band], cl[...])
        )


def increments_of(core, mask, mine, other):
    members = mine.shape[0] * mine.shape[2]
    vmem = pl.BlockSpec(memory_space=pltpu.VMEM)
    return pl.pallas_call(
        enkf_kernel,
        out_shape=jax.ShapeDtypeStruct((members, OWN * TILE), F32),
        in_specs=[pl.BlockSpec(memory_space=pltpu.SMEM), vmem, vmem, vmem],
        out_specs=vmem,
        scratch_shapes=[
            pltpu.VMEM((WINDOW * TILE, members), BF),
            pltpu.VMEM((WINDOW * TILE, members), BF),
            pltpu.VMEM((members, WINDOW * TILE), BF),
            pltpu.VMEM((members, WINDOW * TILE), BF),
            pltpu.VMEM((members, WINDOW * TILE), BF),
            pltpu.VMEM((members, WINDOW * TILE), BF),
            pltpu.VMEM((SPAN * TILE, 2 * TILE), F32),
            pltpu.VMEM((SPAN * TILE, 2 * TILE), BF),
            pltpu.VMEM((SPAN * TILE, 2 * TILE), BF),
        ],
        compiler_params=pltpu.CompilerParams(vmem_limit_bytes=48 * 1024 * 1024),
        cost_estimate=pl.CostEstimate(flops=11_000_000_000, bytes_accessed=9_000_000, transcendentals=0),
    )(core, mask, mine, other)


def keep_mask(neighbours, core, chip, half, regions, rest):
    swap = [(r, r ^ 1) for r in range(regions)]
    theirs = lax.ppermute(neighbours, "region", swap)
    table = jnp.where((chip >= half) == (core == 1), neighbours, theirs)
    start = (chip % half) * CHIP + core * OWN
    lists = lax.dynamic_slice_in_dim(table, start, OWN, 0)
    tiles = neighbours.shape[0] * regions
    region = lax.axis_index("region")
    first = ((region // 2) * 2 + chip // half) * neighbours.shape[0] + start
    spot = (lists - first + HALO) % tiles
    own = jnp.arange(OWN, dtype=jnp.int32).reshape(PAIRS, 1, 2)
    window = own[:, :1, :1] + jnp.arange(SPAN, dtype=jnp.int32).reshape(1, SPAN, 1)
    listed = spot.reshape(PAIRS, 1, 2, -1) == window[..., None]
    keep = jnp.any(listed, axis=-1)
    keep = jnp.where(keep, rest, 0.0).astype(F32)
    return jnp.repeat(keep, TILE, axis=2).reshape(PAIRS * SPAN, 2 * TILE)


def shards(states, weights, obs_count, neighbours):
    chips = lax.axis_size("member")
    regions = lax.axis_size("region")
    rows, local = states.shape
    tiles = local // TILE
    half = chips // 2
    core = lax.axis_index("region") % 2
    chip = lax.axis_index("member")
    up = [(r, (r + 1) % regions) for r in range(regions)]
    down = [(t, s) for s, t in up]
    swap = [(r, r ^ 1) for r in range(regions)]
    rim = HALO * TILE
    counts = obs_count.astype(F32)
    factor = counts / (counts + 8.0)
    scaled = (weights.reshape(rows, tiles, TILE) * factor[None, :, None]).reshape(rows, local)
    stacked = jnp.stack([states, scaled])
    low = lax.ppermute(stacked[:, :, local - rim :], "region", up)
    high = lax.ppermute(stacked[:, :, :rim], "region", down)
    padded = jnp.concatenate([low, stacked, high], axis=2)

    def windows(side):
        if side == 0:
            spans = [(0, PART)]
        else:
            spans = [(PART + HALO, 2 * PART), (PART, PART + HALO)]
        parts = []
        for q in range(half):
            pieces = [padded[:, :, (q * CHIP + a) * TILE : (q * CHIP + b) * TILE] for a, b in spans]
            parts.append(jnp.concatenate(pieces, axis=2) if len(pieces) > 1 else pieces[0])
        return jnp.stack(parts)

    left, right = windows(0), windows(1)
    is_left = core == 0
    keep_here = jnp.where(is_left, left, right)
    send = jnp.where(is_left, right, left)
    got = lax.ppermute(send, "region", swap)
    lower = jnp.where(is_left, keep_here, got)
    upper = jnp.where(is_left, got, keep_here)
    operand = jnp.concatenate([lower, upper], axis=0)
    mine = lax.all_to_all(operand, "member", split_axis=0, concat_axis=0, tiled=True)
    other = lax.ppermute(mine[:, :, :, OWN * TILE :], "region", swap)
    members = chips * rows
    mask = keep_mask(neighbours, core, chip, half, regions, 1.0 / (members - 1.0))
    total = increments_of(core.reshape(1), mask, mine, other)
    back = lax.all_to_all(
        total.reshape(chips, rows, OWN * TILE), "member", split_axis=0, concat_axis=0, tiled=True
    )
    keep_back = jnp.where(is_left, back[:half], back[half:])
    send_back = jnp.where(is_left, back[half:], back[:half])
    got_back = lax.ppermute(send_back, "region", swap)
    first = jnp.where(is_left, keep_back, got_back)
    second = jnp.where(is_left, got_back, keep_back)
    result = jnp.stack([first, second], axis=1)
    return result.transpose(2, 0, 1, 3).reshape(rows, local)


def solution(mesh):
    placed = (P("member", "region"), P("member", "region"), P("region"), P("region", None))
    return jax.shard_map(
        shards, mesh=mesh, in_specs=placed, out_specs=P("member", "region"), check_vma=False
    )
```

time: 551 us -> 165 us (0.30)
  the two profiles are of different devices: /device:TPU:96 before, /device:TPU:1 now
where the time goes in v1:
time: 165 us; the launch traced here: 164 us
  blocking collectives  93.6 us (57%)
  Pallas kernels  28.4 us (17%)
  other arithmetic  13.6 us (8%)
  starting transfers between devices  10.7 us (6%)
  waiting for transfers between devices  9.79 us (6%)
  local copies, waits for them, and re-layouts  8.1 us (5%)
    all_to_all x1, blocking collectives, shards(): lax.all_to_all(operand, 'member', split_axis=0, concat_axis=0, tiled=True)  68.7 us
    pallas_call x1, Pallas kernels, increments_of(): pl.pallas_call(enkf_kernel, out_shape=jax.ShapeDtypeStruct((members, OWN...  28.4 us
    all_to_all x1, blocking collectives, shards(): lax.all_to_all(total.reshape(chips, rows, OWN * TILE), 'member', split_ax...  24.9 us
    unnamed x14, other arithmetic  5.39 us
    ppermute x1, starting transfers between devices, shards(): got = lax.ppermute(send, 'region', swap)  5.38 us
    ppermute x1, waiting for transfers between devices, shards(): got = lax.ppermute(send, 'region', swap)  4.54 us
    ppermute x1, waiting for transfers between devices, keep_mask(): theirs = lax.ppermute(neighbours, 'region', swap)  3.33 us
  transfers between devices with their start and end apart: 6, of which 3 were waited for; matrix products, arithmetic and copies ran while one was open for 4% of the time, Pallas kernels for 0%

profile of v1, /device:TPU:1, one launch (start us, length us, event | category | flops | bytes accessed | tf_op | source)
XLA Modules:
  0.0 164.4 jit_solution(8326397337196408026)
XLA Ops:
  0.0 0.8 add_divide_fusion
  0.9 1.6 multiply_bitcast_fusion
  2.5 0.8 fusion.41
  3.2 3.0 %collective-permute-start.1 = (f32[2,16,1024]{2,1,0:T(8,128)}, f32[2,16,1024]{2,1,0:T(8,128)S(1)}, u32[]{:S(2)}, u32[]{:S(2)}) collective-permute-start(f32[2,16,1024]{2,1,0:T(8,128)} %get-tuple-element.9), channel_id=1, source_target_pairs={{0,1},{1,2},{2,3},{3,4},{4,5},{5,6},{6,7},{7,8},{8,9},{9,10},{10,1... | collective-permute-start | bytes 393224 | tf_op jit(solution)/shard_map/ppermute | solution.py:138
  6.6 0.7 fusion.26
  7.3 0.7 fusion.27
  8.8 0.8 fusion.29
  9.6 0.8 fusion.30
  10.3 0.7 fusion.31
  11.1 0.7 fusion.32
  12.0 0.8 fusion.20
  13.2 5.4 %collective-permute-start.3 = (f32[8,2,16,2560]{3,2,1,0:T(8,128)S(1)}, f32[8,2,16,2560]{3,2,1,0:T(8,128)S(1)}, u32[]{:S(2)}, u32[]{:S(2)}) collective-permute-start(f32[8,2,16,2560]{3,2,1,0:T(8,128)S(1)} %broadcast_select_fusion.2), channel_id=1, source_target_pairs={{0,1},{1,0},{2,3},{3,2},{4,5},{5,4},{6,7},{7,6},{8,9},{9,8},{10,11... | collective-permute-start | bytes 7864328 | tf_op jit(solution)/shard_map/ppermute | solution.py:157
  18.6 4.5 %collective-permute-done.3 = f32[8,2,16,2560]{3,2,1,0:T(8,128)S(1)} collective-permute-done((f32[8,2,16,2560]{3,2,1,0:T(8,128)S(1)}, f32[8,2,16,2560]{3,2,1,0:T(8,128)S(1)}, u32[]{:S(2)}, u32[]{:S(2)}) %collective-permute-start.3) | collective-permute-done | bytes 2621472 | tf_op jit(solution)/shard_map/ppermute | solution.py:157
  23.1 2.6 %broadcast_select_fusion.1 = (f32[8,2,16,2560]{3,2,1,0:T(8,128)S(1)}, f32[8,2,16,2560]{3,2,1,0:T(8,128)S(1)}) fusion(f32[8,2,16,2560]{3,2,1,0:T(8,128)S(1)} %collective-permute-done.3, pred[]{:T(512)S(6)} %eq.29, f32[8,2,16,2560]{3,2,1,0:T(8,128)S(1)} %get-tuple-element.7, f32[8,2,16,2560]{3,2,1,0:T(8,128)} %get-tuple-element.8), kind=kLoop, calls=%fused_computation.50 | loop fusion | flops 1966080 | bytes 13107201 | tf_op jit(solution)/shard_map/jit(_where)/select_n | solution.py:158
  26.3 68.7 %all_to_all.10.mine_ref = f32[16,2,16,2560]{3,2,1,0:T(8,128)S(1)} all-to-all(f32[16,2,16,2560]{3,2,1,0:T(8,128)S(1)} %pad_maximum_fusion), channel_id=1, replica_groups=mesh['member'=16,'region'=16] {'member'}, dimensions={0} | all-to-all | bytes 10485760 | tf_op jit(solution)/shard_map/all_to_all | solution.py:161
  94.9 2.3 %copy-done.1 = f32[16,2,16,2560]{3,2,1,0:T(8,128)} copy-done((f32[16,2,16,2560]{3,2,1,0:T(8,128)}, f32[16,2,16,2560]{3,2,1,0:T(8,128)S(1)}, u32[]{:S(2)}) %copy-start.1) | copy-done | bytes 5242904
  97.2 1.5 slice.170
  99.4 3.3 %collective-permute-done = s32[192,12]{0,1:T(8,128)S(1)} collective-permute-done((s32[192,12]{0,1:T(8,128)S(1)}, s32[192,12]{0,1:T(8,128)S(1)}, u32[]{:S(2)}, u32[]{:S(2)}) %collective-permute-start) | collective-permute-done | bytes 9248 | tf_op jit(solution)/shard_map/ppermute | solution.py:106
  103.4 28.4 %shard_map.46 = f32[256,1536]{1,0:T(8,128)S(1)} custom-call(s32[1]{0:T(128)} %bitcast.core_ref, f32[108,256]{1,0:T(8,128)S(1)} %bitcast.84, f32[16,2,16,2560]{3,2,1,0:T(8,128)} %copy-done.1, f32[16,2,16,1024]{3,2,1,0:T(8,128)S(1)} %collective-permute-done.4.other_ref), custom_call_target="tpu_custom_call" | custom-call | flops 11000000512 | bytes 9000000 | tf_op jit(solution)/shard_map/pallas_call | solution.py:83
  131.8 24.9 %all_to_all.11 = f32[16,16,1536]{2,1,0:T(8,128)S(1)} all-to-all(f32[16,16,1536]{2,1,0:T(8,128)S(1)} %bitcast.83), channel_id=1, replica_groups=mesh['member'=16,'region'=16] {'member'}, dimensions={0} | all-to-all | bytes 3145728 | tf_op jit(solution)/shard_map/all_to_all | solution.py:166
  156.8 1.6 collective-permute-start.5
  158.4 1.9 %collective-permute-done.5 = f32[8,16,1536]{2,1,0:T(8,128)S(1)} collective-permute-done((f32[8,16,1536]{2,1,0:T(8,128)S(1)}, f32[8,16,1536]{2,1,0:T(8,128)S(1)}, u32[]{:S(2)}, u32[]{:S(2)}) %collective-permute-start.5) | collective-permute-done | bytes 786464 | tf_op jit(solution)/shard_map/ppermute | solution.py:171
  160.6 1.2 copy.11
  161.9 2.5 %reshape.82 = f32[16,24576]{1,0:T(8,128)} reshape(f32[16,8,2,1536]{3,2,1,0:T(2,128)S(1)} %copy.11) | data formatting | bytes 3145728 | tf_op jit(solution)/shard_map/reshape | solution.py:175
  (38 shorter events, 3.9 us)
Async XLA Ops:
  0.0 2.5 %copy-start = (f32[16,24576]{1,0:T(8,128)S(1)}, f32[16,24576]{1,0:T(8,128)}, u32[]{:S(2)}) copy-start(f32[16,24576]{1,0:T(8,128)} %param.4) | copy-start | bytes 4718596
  3.2 8.6 %collective-permute-start.1 = (f32[2,16,1024]{2,1,0:T(8,128)}, f32[2,16,1024]{2,1,0:T(8,128)S(1)}, u32[]{:S(2)}, u32[]{:S(2)}) collective-permute-start(f32[2,16,1024]{2,1,0:T(8,128)} %get-tuple-element.9), channel_id=1, source_target_pairs={{0,1},{1,2},{2,3},{3,4},{4,5},{5,6},{6,7},{7,8},{8,9},{9,10},{10,1... | collective-permute-start | bytes 393224 | tf_op jit(solution)/shard_map/ppermute | solution.py:138
  6.3 5.8 %collective-permute-start.2 = (f32[2,16,1024]{2,1,0:T(8,128)S(1)}, f32[2,16,1024]{2,1,0:T(8,128)S(1)}, u32[]{:S(2)}, u32[]{:S(2)}) collective-permute-start(f32[2,16,1024]{2,1,0:T(8,128)S(1)} %get-tuple-element.17), channel_id=1, source_target_pairs={{1,0},{2,1},{3,2},{4,3},{5,4},{6,5},{7,6},{8,7},{9,8},{10,9},{11,1... | collective-permute-start | bytes 393224 | tf_op jit(solution)/shard_map/ppermute | solution.py:139
  13.2 9.9 %collective-permute-start.3 = (f32[8,2,16,2560]{3,2,1,0:T(8,128)S(1)}, f32[8,2,16,2560]{3,2,1,0:T(8,128)S(1)}, u32[]{:S(2)}, u32[]{:S(2)}) collective-permute-start(f32[8,2,16,2560]{3,2,1,0:T(8,128)S(1)} %broadcast_select_fusion.2), channel_id=1, source_target_pairs={{0,1},{1,0},{2,3},{3,2},{4,5},{5,4},{6,7},{7,6},{8,9},{9,8},{10,11... | collective-permute-start | bytes 7864328 | tf_op jit(solution)/shard_map/ppermute | solution.py:157
  94.9 2.3 %copy-start.1 = (f32[16,2,16,2560]{3,2,1,0:T(8,128)}, f32[16,2,16,2560]{3,2,1,0:T(8,128)S(1)}, u32[]{:S(2)}) copy-start(f32[16,2,16,2560]{3,2,1,0:T(8,128)S(1)} %all_to_all.10.mine_ref) | copy-start | bytes 15728644
  97.2 1.7 %copy-start.2 = (s32[192,12]{0,1:T(8,128)S(1)}, s32[192,12]{0,1:T(8,128)}, u32[]{:S(2)}) copy-start(s32[192,12]{0,1:T(8,128)} %param.7) | copy-start | bytes 27652
  98.8 4.6 %collective-permute-start.4 = (f32[16,2,16,1024]{3,2,1,0:T(8,128)}, f32[16,2,16,1024]{3,2,1,0:T(8,128)S(1)}, u32[]{:S(2)}, u32[]{:S(2)}) collective-permute-start(f32[16,2,16,1024]{3,2,1,0:T(8,128)} %slice.170), channel_id=1, source_target_pairs={{0,1},{1,0},{2,3},{3,2},{4,5},{5,4},{6,7},{7,6},{8,9},{9,8},{10,11... | collective-permute-start | bytes 6291464 | tf_op jit(solution)/shard_map/ppermute | solution.py:162
  98.9 3.8 %collective-permute-start = (s32[192,12]{0,1:T(8,128)S(1)}, s32[192,12]{0,1:T(8,128)S(1)}, u32[]{:S(2)}, u32[]{:S(2)}) collective-permute-start(s32[192,12]{0,1:T(8,128)S(1)} %copy-done.2), channel_id=1, source_target_pairs={{0,1},{1,0},{2,3},{3,2},{4,5},{5,4},{6,7},{7,6},{8,9},{9,8},{10,11... | collective-permute-start | bytes 27656 | tf_op jit(solution)/shard_map/ppermute | solution.py:106
  156.8 3.5 %collective-permute-start.5 = (f32[8,16,1536]{2,1,0:T(8,128)S(1)}, f32[8,16,1536]{2,1,0:T(8,128)S(1)}, u32[]{:S(2)}, u32[]{:S(2)}) collective-permute-start(f32[8,16,1536]{2,1,0:T(8,128)S(1)} %slice_select_fusion), channel_id=1, source_target_pairs={{0,1},{1,0},{2,3},{3,2},{4,5},{5,4},{6,7},{7,6},{8,9},{9,8},{10,11... | collective-permute-start | bytes 2359304 | tf_op jit(solution)/shard_map/ppermute | solution.py:171

commit v2 on v1

v2 whole, which is shorter than its diff:
```python
import jax
import jax.numpy as jnp
from jax import lax
from jax.experimental import pallas as pl
from jax.experimental.pallas import tpu as pltpu
from jax.sharding import PartitionSpec as P

TILE = 128
HALO = 8
OWN = 12
CHIP = 2 * OWN
WINDOW = OWN + 2 * HALO
PAIRS = OWN // 2
SPAN = 2 * HALO + 2
BF = jnp.bfloat16
F32 = jnp.float32
MIB = 1024 * 1024
VMEM = pl.BlockSpec(memory_space=pltpu.VMEM)
SMEM = pl.BlockSpec(memory_space=pltpu.SMEM)


def split(x):
    high = x.astype(BF)
    return high, (x - high.astype(F32)).astype(BF)


def dot(a, b):
    return jnp.dot(a, b, preferred_element_type=F32)


def cols(start, count=1):
    return slice(start * TILE, (start + count) * TILE)


def lanes(t, count=1):
    return pl.ds(pl.multiple_of(t * TILE, TILE), count * TILE)


def send_kernel(core_ref, counts_ref, states_ref, weights_ref, scaled_ref, out_ref):
    half = out_ref.shape[0]

    @pl.loop(0, half * CHIP // 8)
    def _(group):
        for lane in range(8):
            t = group * 8 + lane
            count = jnp.full((1, TILE), counts_ref[t], jnp.int32).astype(F32)
            scaled_ref[:, lanes(t)] = weights_ref[:, lanes(t)] * (count / (count + 8.0))

    rows = states_ref.shape[0]
    for ref, there in ((states_ref, slice(0, rows)), (scaled_ref, slice(rows, None))):

        @pl.when(core_ref[0] == 0)
        def _(ref=ref, there=there):
            for q in range(half):
                for t in range(OWN):
                    out_ref[q, there, cols(t)] = ref[:, cols((q + 1) * CHIP - 1 - t)]

        @pl.when(core_ref[0] != 0)
        def _(ref=ref, there=there):
            for q in range(half):
                out_ref[q, there, cols(0, OWN)] = ref[:, cols(q * CHIP, OWN)]


def merge_kernel(core_ref, states_ref, scaled_ref, got_ref, out_ref):
    half = got_ref.shape[0]
    rows = states_ref.shape[0]

    @pl.when(core_ref[0] == 0)
    def _():
        for q in range(half):
            out_ref[q, :rows, :] = states_ref[:, cols(q * CHIP, OWN)]
            out_ref[q, rows:, :] = scaled_ref[:, cols(q * CHIP, OWN)]
            out_ref[half + q] = got_ref[q]

    @pl.when(core_ref[0] != 0)
    def _():
        for q in range(half):
            for t in range(OWN):
                out_ref[half + q, :rows, cols(t)] = states_ref[:, cols((q + 1) * CHIP - 1 - t)]
                out_ref[half + q, rows:, cols(t)] = scaled_ref[:, cols((q + 1) * CHIP - 1 - t)]
            out_ref[q] = got_ref[q]


def place_kernel(core_ref, back_ref, got_ref, out_ref):
    half = got_ref.shape[0]

    @pl.when(core_ref[0] == 0)
    def _():
        for q in range(half):
            out_ref[:, cols(q * CHIP, OWN)] = back_ref[q]
            for t in range(OWN):
                out_ref[:, cols((q + 1) * CHIP - 1 - t)] = got_ref[q, :, cols(t)]

    @pl.when(core_ref[0] != 0)
    def _():
        for q in range(half):
            out_ref[:, cols(q * CHIP, OWN)] = got_ref[q]
            for t in range(OWN):
                out_ref[:, cols((q + 1) * CHIP - 1 - t)] = back_ref[half + q, :, cols(t)]


def anomaly_of(ref, t, members):
    rows = members // ref.shape[0]
    state = ref[:, :rows, lanes(t)].reshape(members, TILE)
    return state - jnp.sum(state, axis=0, keepdims=True) * (1.0 / members)


def place_window(ref, t, w, members, ath, atl, both):
    ath[lanes(w), :], atl[lanes(w), :] = split(anomaly_of(ref, t, members).T)
    weights = ref[:, members // ref.shape[0] :, lanes(t)].reshape(members, TILE)
    both[:members, lanes(w)], both[members:, lanes(w)] = split(weights)


def place_own(ref, t, members, ah, al):
    ah[:, lanes(t)], al[:, lanes(t)] = split(anomaly_of(ref, t, members))


def place_taper(core, count, taper):
    sign = jnp.where(core == 0, TILE, -TILE)

    @pl.loop(0, count)
    def _(k):
        down = lax.broadcasted_iota(jnp.int32, (TILE, 2 * TILE), 0)
        across = lax.broadcasted_iota(jnp.int32, (TILE, 2 * TILE), 1)
        second = (across >= TILE).astype(jnp.int32)
        spread = sign * (k - HALO - second) + down - (across - TILE * second)
        scaled = spread.astype(F32) / (2.0 * TILE)
        taper[lanes(k), :] = 1.0 / (1.0 + scaled * scaled)


def products(pair, first, last, skip, mask_ref, ah, al, ath, atl, both, taper, ch, cl):
    members = ah.shape[0]
    own_high, own_low = ah[:, cols(2 * pair, 2)], al[:, cols(2 * pair, 2)]
    slot = pair % 2
    for k in range(first, last, 2):
        there = cols(2 * pair + k - skip, 2)
        high = ath[there, :]
        covar = dot(high, own_high) + (dot(atl[there, :], own_high) + dot(high, own_low))
        covar = covar * taper[cols(k, 2), :]
        for half in range(2):
            keep = mask_ref[pair * SPAN + k + half : pair * SPAN + k + half + 1, :]
            coefficient = covar[half * TILE : (half + 1) * TILE] * keep
            ch[slot, cols(k + half), :], cl[slot, cols(k + half), :] = split(coefficient)
    band = cols(2 * pair + first - skip, last - first)
    high, low = ch[slot, cols(first, last - first), :], cl[slot, cols(first, last - first), :]
    total = dot(both[:, band], high)
    return total[:members] + (total[members:] + dot(both[:members, band], low))


def near_kernel(core_ref, mask_ref, mine_ref, other_ref, out_ref, ah, al, ath, atl, both, taper, ch, cl):
    members = ah.shape[0]

    @pl.loop(0, OWN)
    def _(t):
        place_window(mine_ref, t, t, members, ath, atl, both)
        place_own(mine_ref, t, members, ah, al)

    @pl.loop(0, HALO)
    def _(t):
        place_window(other_ref, t, OWN + HALO - 1 - t, members, ath, atl, both)

    place_taper(core_ref[0], SPAN, taper)
    for pair in range(PAIRS):
        first = max(0, HALO - 2 * pair)
        out_ref[:, cols(2 * pair, 2)] = products(
            pair, first, SPAN, HALO, mask_ref, ah, al, ath, atl, both, taper, ch, cl
        )


def far_kernel(core_ref, mask_ref, mine_ref, halo_ref, near_ref, out_ref, ah, al, ath, atl, both, taper, ch, cl):
    members = ah.shape[0]

    @pl.loop(0, HALO)
    def _(t):
        place_window(halo_ref, t, HALO - 1 - t, members, ath, atl, both)
        place_own(mine_ref, t, members, ah, al)

    place_taper(core_ref[0], HALO, taper)
    for pair in range(PAIRS):
        there = cols(2 * pair, 2)
        last = HALO - 2 * pair
        if last > 0:
            out_ref[:, there] = near_ref[:, there] + products(
                pair, 0, last, 0, mask_ref, ah, al, ath, atl, both, taper, ch, cl
            )
        else:
            out_ref[:, there] = near_ref[:, there]


def windowed(kernel, members, own, window, span, flops, name):
    return pl.pallas_call(
        kernel,
        out_shape=jax.ShapeDtypeStruct((members, OWN * TILE), F32),
        in_specs=[SMEM, VMEM, VMEM, VMEM] + [VMEM] * (name == "far"),
        out_specs=VMEM,
        scratch_shapes=[
            pltpu.VMEM((members, own * TILE), BF),
            pltpu.VMEM((members, own * TILE), BF),
            pltpu.VMEM((window * TILE, members), BF),
            pltpu.VMEM((window * TILE, members), BF),
            pltpu.VMEM((2 * members, window * TILE), BF),
            pltpu.VMEM((span * TILE, 2 * TILE), F32),
            pltpu.VMEM((2, span * TILE, 2 * TILE), BF),
            pltpu.VMEM((2, span * TILE, 2 * TILE), BF),
        ],
        compiler_params=pltpu.CompilerParams(vmem_limit_bytes=32 * MIB),
        cost_estimate=pl.CostEstimate(flops=flops, bytes_accessed=8_000_000, transcendentals=0),
        name=name,
    )


def copying(kernel, outs, ins, name):
    return pl.pallas_call(
        kernel,
        out_shape=outs,
        in_specs=ins,
        out_specs=jax.tree.map(lambda _: VMEM, outs),
        compiler_params=pltpu.CompilerParams(vmem_limit_bytes=14 * MIB),
        cost_estimate=pl.CostEstimate(flops=0, bytes_accessed=6_000_000, transcendentals=0),
        name=name,
    )


def keep_mask(neighbours, core, chip, half, regions, value):
    theirs = lax.ppermute(neighbours, "region", [(r, r ^ 1) for r in range(regions)])
    table = jnp.where((chip >= half) == (core == 1), neighbours, theirs)
    start = (chip % half) * CHIP + core * OWN
    lists = lax.dynamic_slice_in_dim(table, start, OWN, 0)
    tiles = neighbours.shape[0] * regions
    region = lax.axis_index("region")
    first = ((region // 2) * 2 + chip // half) * neighbours.shape[0] + start
    spot = (lists - first + HALO) % tiles
    spot = jnp.where(core == 0, spot, WINDOW - 1 - spot[::-1])
    own = jnp.arange(OWN, dtype=jnp.int32).reshape(PAIRS, 1, 2)
    window = own[:, :1, :1] + jnp.arange(SPAN, dtype=jnp.int32).reshape(1, SPAN, 1)
    keep = jnp.any(spot.reshape(PAIRS, 1, 2, -1) == window[..., None], axis=-1)
    keep = jnp.where(keep, value, 0.0).astype(F32)
    return jnp.repeat(keep, TILE, axis=2).reshape(PAIRS * SPAN, 2 * TILE)


def outward(chips, regions):
    pairs = []
    for chip in range(chips):
        for region in range(regions):
            plane, core = region // 2, region % 2
            place = (plane * chips + chip + (1 if core else -1)) % (chips * regions // 2)
            pairs.append((chip * regions + region, place % chips * regions + place // chips * 2 + 1 - core))
    return pairs


def shards(states, weights, obs_count, neighbours):
    chips = lax.axis_size("member")
    regions = lax.axis_size("region")
    rows, local = states.shape
    half = chips // 2
    core = lax.axis_index("region") % 2
    chip = lax.axis_index("member")
    swap = [(r, r ^ 1) for r in range(regions)]
    members = chips * rows
    flag = core.reshape(1)
    own = OWN * TILE

    scaled, sent = copying(
        send_kernel,
        (jax.ShapeDtypeStruct((rows, local), F32), jax.ShapeDtypeStruct((half, 2 * rows, own), F32)),
        [SMEM, SMEM, VMEM, VMEM],
        "send",
    )(flag, obs_count, states, weights)
    got = lax.ppermute(sent, "region", swap)
    operand = copying(
        merge_kernel,
        jax.ShapeDtypeStruct((chips, 2 * rows, own), F32),
        [SMEM, VMEM, VMEM, VMEM],
        "merge",
    )(flag, states, scaled, got)
    mask = keep_mask(neighbours, core, chip, half, regions, 1.0 / (members - 1.0))
    operand, mask = lax.optimization_barrier((operand, mask))
    mine = lax.all_to_all(operand, "member", split_axis=0, concat_axis=0, tiled=True)
    halo = lax.ppermute(mine[:, :, : HALO * TILE], ("member", "region"), outward(chips, regions))
    other = lax.ppermute(mine[:, :, own - HALO * TILE :], "region", swap)
    near = windowed(near_kernel, members, OWN, OWN + HALO, SPAN, 18_000_000_000, "near")(flag, mask, mine, other)
    total = windowed(far_kernel, members, HALO, HALO, HALO, 4_000_000_000, "far")(flag, mask, mine, halo, near)
    back = lax.all_to_all(total.reshape(chips, rows, own), "member", split_axis=0, concat_axis=0, tiled=True)
    got = lax.ppermute(jnp.where(core == 0, back[half:], back[:half]), "region", swap)
    return copying(
        place_kernel, jax.ShapeDtypeStruct((rows, local), F32), [SMEM, VMEM, VMEM], "place"
    )(flag, back, got)


def solution(mesh):
    placed = (P("member", "region"), P("member", "region"), P("region"), P("region", None))
    return jax.shard_map(
        shards, mesh=mesh, in_specs=placed, out_specs=P("member", "region"), check_vma=False
    )
```

time: 165 us -> 125 us (0.76)
  blocking collectives: 93.6 us -> 71.2 us
  other arithmetic: 13.6 us -> 0.38 us
  waiting for transfers between devices: 9.79 us -> 16 us
  Pallas kernels: 28.4 us -> 23.4 us
  local copies, waits for them, and re-layouts: 8.1 us -> 4.48 us
  starting transfers between devices: 10.7 us -> 8.34 us
    all_to_all x1, blocking collectives: 68.7 us -> 44 us  [shards(): lax.all_to_all(operand, 'member', split_axis=0, concat_axis=0, tiled=True)]
    ppermute x6 -> x5, waiting for transfers between devices: 9.79 us -> 16 us  [the longest x1 7.88 us: shards(): lax.ppermute(mine[:, :, :HALO * TILE], ('member', 'region'), outward(chip...]
    unnamed x14 -> x0, other arithmetic: 5.39 us -> none
    pallas_call x1 -> x5, Pallas kernels: 28.4 us -> 23.4 us  [the longest x1 14.1 us: shards(): windowed(near_kernel, members, OWN, OWN + HALO, SPAN, 18000000000, 'near')]
    select_n x4 -> x3, other arithmetic: 3.06 us -> 0.1 us  [the longest x1 0.09 us: shards(): jnp.where(core == 0, back[half:], back[:half])]
    reshape x1 -> x0, local copies, waits for them, and re-layouts: 2.49 us -> none  [shards(): return result.transpose(2, 0, 1, 3).reshape(rows, local)]
    ppermute x6 -> x5, starting transfers between devices: 10.7 us -> 8.34 us  [the longest x1 3.24 us: shards(): got = lax.ppermute(sent, 'region', swap)]
    all_to_all x1, blocking collectives: 24.9 us -> 27.2 us  [shards(): lax.all_to_all(total.reshape(chips, rows, own), 'member', split_axis=0, c...]
  transfers between devices with their start and end apart: 6 -> 5, of which waited for: 3 -> 4; matrix products, arithmetic and copies ran while one was open for 4% -> 1% of each run, Pallas kernels for 0% -> 11%
where the time goes in v2:
time: 125 us; the launch traced here: 124 us
  blocking collectives  71.2 us (57%)
  Pallas kernels  23.4 us (19%)
  waiting for transfers between devices  16 us (13%)
  starting transfers between devices  8.34 us (7%)
  local copies, waits for them, and re-layouts  4.48 us (4%)
    all_to_all x1, blocking collectives, shards(): lax.all_to_all(operand, 'member', split_axis=0, concat_axis=0, tiled=True)  44 us
    all_to_all x1, blocking collectives, shards(): lax.all_to_all(total.reshape(chips, rows, own), 'member', split_axis=0, c...  27.2 us
    pallas_call x1, Pallas kernels, shards(): windowed(near_kernel, members, OWN, OWN + HALO, SPAN, 18000000000, 'near')  14.1 us
    ppermute x1, waiting for transfers between devices, shards(): lax.ppermute(mine[:, :, :HALO * TILE], ('member', 'region'), outward(chip...  7.88 us
    pallas_call x1, Pallas kernels, shards(): windowed(far_kernel, members, HALO, HALO, HALO, 4000000000, 'far')  4.1 us
    unnamed x12, local copies, waits for them, and re-layouts  3.55 us
    ppermute x1, waiting for transfers between devices, shards(): other = lax.ppermute(mine[:, :, own - HALO * TILE:], 'region', swap)  3.34 us
    ppermute x1, starting transfers between devices, shards(): got = lax.ppermute(sent, 'region', swap)  3.24 us
  transfers between devices with their start and end apart: 5, of which 4 were waited for; matrix products, arithmetic and copies ran while one was open for 1% of the time, Pallas kernels for 11%

profile of v2, /device:TPU:1, one launch (start us, length us, event | category | flops | bytes accessed | tf_op | source)
XLA Modules:
  0.0 123.9 jit_solution(2384690310018808827)
XLA Ops:
  0.0 1.4 %copy-done = f32[16,24576]{1,0:T(8,128)S(1)} copy-done((f32[16,24576]{1,0:T(8,128)S(1)}, f32[16,24576]{1,0:T(8,128)}, u32[]{:S(2)}) %copy-start) | copy-done | bytes 1572888
  1.4 1.4 %copy-done.2 = f32[16,24576]{1,0:T(8,128)S(1)} copy-done((f32[16,24576]{1,0:T(8,128)S(1)}, f32[16,24576]{1,0:T(8,128)}, u32[]{:S(2)}) %copy-start.2) | copy-done | bytes 1572888
  2.8 0.7 copy-done.3
  3.5 2.3 %send.1 = (f32[16,24576]{1,0:T(8,128)S(1)}, f32[8,32,1536]{2,1,0:T(8,128)}) custom-call(s32[1]{0:T(128)} %bitcast.core_ref, s32[192]{0:T(256)S(1)} %copy-done.3, f32[16,24576]{1,0:T(8,128)S(1)} %copy-done, f32[16,24576]{1,0:T(8,128)S(1)} %copy-done.2), custom_call_target="tpu_custom_call" | custom-call | bytes 6000000 | tf_op jit(solution)/shard_map/send/pallas_call | solution.py:263
  5.8 3.2 %collective-permute-start = (f32[8,32,1536]{2,1,0:T(8,128)}, f32[8,32,1536]{2,1,0:T(8,128)}, u32[]{:S(2)}, u32[]{:S(2)}) collective-permute-start(f32[8,32,1536]{2,1,0:T(8,128)} %get-tuple-element.10), channel_id=1, source_target_pairs={{0,1},{1,0},{2,3},{3,2},{4,5},{5,4},{6,7},{7,6},{8,9},{9,8},{10,11... | collective-permute-start | bytes 4718600 | tf_op jit(solution)/shard_map/ppermute | solution.py:269
  9.2 2.8 %collective-permute-done.1 = s32[192,12]{0,1:T(8,128)S(1)} collective-permute-done((s32[192,12]{0,1:T(8,128)S(1)}, s32[192,12]{0,1:T(8,128)S(1)}, u32[]{:S(2)}, u32[]{:S(2)}) %collective-permute-start.1) | collective-permute-done | bytes 9248 | tf_op jit(solution)/shard_map/ppermute | solution.py:225
  12.2 0.1 copy.7
  12.3 0.1 compare_reduce_fusion
  12.4 0.1 copy.8
  12.6 0.2 broadcast_in_dim.14
  12.8 1.6 %merge.1 = f32[16,32,1536]{2,1,0:T(8,128)S(1)} custom-call(s32[1]{0:T(128)} %bitcast.core_ref, f32[16,24576]{1,0:T(8,128)S(1)} %copy-done.1, f32[16,24576]{1,0:T(8,128)S(1)} %get-tuple-element.9.scaled_ref, f32[8,32,1536]{2,1,0:T(8,128)} %collective-permute-done.got_ref), custom_call_target="tpu_custom_call" | custom-call | bytes 6000000 | tf_op jit(solution)/shard_map/merge/pallas_call | solution.py:270
  14.4 44.0 %all_to_all.10.mine_ref = f32[16,32,1536]{2,1,0:T(8,128)S(1)} all-to-all(f32[16,32,1536]{2,1,0:T(8,128)S(1)} %merge.1), channel_id=1, replica_groups=mesh['member'=16,'region'=16] {'member'}, dimensions={0} | all-to-all | bytes 6291456 | tf_op jit(solution)/shard_map/all_to_all | solution.py:278
  58.5 0.4 fusion.3
  58.9 1.7 %collective-permute-start.3 = (f32[16,32,1024]{2,1,0:T(8,128)S(1)}, f32[16,32,1024]{2,1,0:T(8,128)S(1)}, u32[]{:S(2)}, u32[]{:S(2)}) collective-permute-start(f32[16,32,1024]{2,1,0:T(8,128)S(1)} %get-tuple-element.13), channel_id=1, source_target_pairs={{0,1},{1,0},{2,3},{3,2},{4,5},{5,4},{6,7},{7,6},{8,9},{9,8},{10,11... | collective-permute-start | bytes 6291464 | tf_op jit(solution)/shard_map/ppermute | solution.py:280
  60.6 0.5 collective-permute-start.2
  61.0 3.3 %collective-permute-done.3.other_ref = f32[16,32,1024]{2,1,0:T(8,128)S(1)} collective-permute-done((f32[16,32,1024]{2,1,0:T(8,128)S(1)}, f32[16,32,1024]{2,1,0:T(8,128)S(1)}, u32[]{:S(2)}, u32[]{:S(2)}) %collective-permute-start.3) | collective-permute-done | bytes 2097184 | tf_op jit(solution)/shard_map/ppermute | solution.py:280
  64.4 14.1 %near.1.near_ref = f32[256,1536]{1,0:T(8,128)S(1)} custom-call(s32[1]{0:T(128)} %bitcast.core_ref, f32[108,256]{1,0:T(8,128)S(1)} %bitcast.9, f32[16,32,1536]{2,1,0:T(8,128)S(1)} %all_to_all.10.mine_ref, f32[16,32,1024]{2,1,0:T(8,128)S(1)} %collective-permute-done.3.other_ref), custom_call_target="tpu_custom_call" | custom-call | flops 17999998976 | bytes 8000000 | tf_op jit(solution)/shard_map/near/pallas_call | solution.py:281
  78.5 7.9 %collective-permute-done.2.halo_ref = f32[16,32,1024]{2,1,0:T(8,128)S(1)} collective-permute-done((f32[16,32,1024]{2,1,0:T(8,128)S(1)}, f32[16,32,1024]{2,1,0:T(8,128)S(1)}, u32[]{:S(2)}, u32[]{:S(2)}) %collective-permute-start.2) | collective-permute-done | bytes 2097184 | tf_op jit(solution)/shard_map/ppermute | solution.py:279
  86.3 4.1 %far.1 = f32[256,1536]{1,0:T(8,128)S(1)} custom-call(s32[1]{0:T(128)} %bitcast.core_ref, f32[108,256]{1,0:T(8,128)S(1)} %bitcast.10, f32[16,32,1536]{2,1,0:T(8,128)S(1)} %all_to_all.10.mine_ref, f32[16,32,1024]{2,1,0:T(8,128)S(1)} %collective-permute-done.2.halo_ref, f32[256,1536]{1,0:T(8,128)S(1)} %near.1.near_ref), custom_call_target="tpu_custom_call" | custom-call | flops 4000000000 | bytes 8000000 | tf_op jit(solution)/shard_map/far/pallas_call | solution.py:282
  90.4 27.2 %all_to_all.11.back_ref = f32[16,16,1536]{2,1,0:T(8,128)S(1)} all-to-all(f32[16,16,1536]{2,1,0:T(8,128)S(1)} %bitcast.8), channel_id=1, replica_groups=mesh['member'=16,'region'=16] {'member'}, dimensions={0} | all-to-all | bytes 3145728 | tf_op jit(solution)/shard_map/all_to_all | solution.py:283
  117.6 0.1 slice_select_fusion
  117.7 3.0 %collective-permute-start.4 = (f32[8,16,1536]{2,1,0:T(8,128)S(1)}, f32[8,16,1536]{2,1,0:T(8,128)S(1)}, u32[]{:S(2)}, u32[]{:S(2)}) collective-permute-start(f32[8,16,1536]{2,1,0:T(8,128)S(1)} %slice_select_fusion), channel_id=1, source_target_pairs={{0,1},{1,0},{2,3},{3,2},{4,5},{5,4},{6,7},{7,6},{8,9},{9,8},{10,11... | collective-permute-start | bytes 2359304 | tf_op jit(solution)/shard_map/ppermute | solution.py:284
  120.7 1.9 %collective-permute-done.4.got_ref = f32[8,16,1536]{2,1,0:T(8,128)S(1)} collective-permute-done((f32[8,16,1536]{2,1,0:T(8,128)S(1)}, f32[8,16,1536]{2,1,0:T(8,128)S(1)}, u32[]{:S(2)}, u32[]{:S(2)}) %collective-permute-start.4) | collective-permute-done | bytes 786464 | tf_op jit(solution)/shard_map/ppermute | solution.py:284
  122.6 1.2 %place.1 = f32[16,24576]{1,0:T(8,128)} custom-call(s32[1]{0:T(128)} %bitcast.core_ref, f32[16,16,1536]{2,1,0:T(8,128)S(1)} %all_to_all.11.back_ref, f32[8,16,1536]{2,1,0:T(8,128)S(1)} %collective-permute-done.4.got_ref), custom_call_target="tpu_custom_call" | custom-call | bytes 6000000 | tf_op jit(solution)/shard_map/place/pallas_call | solution.py:285
  (19 shorter events, 0.3 us)
Async XLA Ops:
  0.0 1.4 %copy-start = (f32[16,24576]{1,0:T(8,128)S(1)}, f32[16,24576]{1,0:T(8,128)}, u32[]{:S(2)}) copy-start(f32[16,24576]{1,0:T(8,128)} %states_ref.3) | copy-start | bytes 4718596
  1.4 1.4 %copy-start.2 = (f32[16,24576]{1,0:T(8,128)S(1)}, f32[16,24576]{1,0:T(8,128)}, u32[]{:S(2)}) copy-start(f32[16,24576]{1,0:T(8,128)} %weights_ref.1) | copy-start | bytes 4718596
  2.8 0.7 copy-start.3
  3.5 5.6 %copy-start.4 = (s32[192,12]{0,1:T(8,128)S(1)}, s32[192,12]{0,1:T(8,128)}, u32[]{:S(2)}) copy-start(s32[192,12]{0,1:T(8,128)} %param.7) | copy-start | bytes 27652
  3.5 9.3 %copy-start.1 = (f32[16,24576]{1,0:T(8,128)S(1)}, f32[16,24576]{1,0:T(8,128)}, u32[]{:S(2)}) copy-start(f32[16,24576]{1,0:T(8,128)} %states_ref.3) | copy-start | bytes 4718596
  5.8 7.0 %collective-permute-start = (f32[8,32,1536]{2,1,0:T(8,128)}, f32[8,32,1536]{2,1,0:T(8,128)}, u32[]{:S(2)}, u32[]{:S(2)}) collective-permute-start(f32[8,32,1536]{2,1,0:T(8,128)} %get-tuple-element.10), channel_id=1, source_target_pairs={{0,1},{1,0},{2,3},{3,2},{4,5},{5,4},{6,7},{7,6},{8,9},{9,8},{10,11... | collective-permute-start | bytes 4718600 | tf_op jit(solution)/shard_map/ppermute | solution.py:269
  9.1 2.9 %collective-permute-start.1 = (s32[192,12]{0,1:T(8,128)S(1)}, s32[192,12]{0,1:T(8,128)S(1)}, u32[]{:S(2)}, u32[]{:S(2)}) collective-permute-start(s32[192,12]{0,1:T(8,128)S(1)} %copy-done.4), channel_id=1, source_target_pairs={{0,1},{1,0},{2,3},{3,2},{4,5},{5,4},{6,7},{7,6},{8,9},{9,8},{10,11... | collective-permute-start | bytes 27656 | tf_op jit(solution)/shard_map/ppermute | solution.py:225
  58.9 5.4 %collective-permute-start.3 = (f32[16,32,1024]{2,1,0:T(8,128)S(1)}, f32[16,32,1024]{2,1,0:T(8,128)S(1)}, u32[]{:S(2)}, u32[]{:S(2)}) collective-permute-start(f32[16,32,1024]{2,1,0:T(8,128)S(1)} %get-tuple-element.13), channel_id=1, source_target_pairs={{0,1},{1,0},{2,3},{3,2},{4,5},{5,4},{6,7},{7,6},{8,9},{9,8},{10,11... | collective-permute-start | bytes 6291464 | tf_op jit(solution)/shard_map/ppermute | solution.py:280
  60.6 25.8 %collective-permute-start.2 = (f32[16,32,1024]{2,1,0:T(8,128)S(1)}, f32[16,32,1024]{2,1,0:T(8,128)S(1)}, u32[]{:S(2)}, u32[]{:S(2)}) collective-permute-start(f32[16,32,1024]{2,1,0:T(8,128)S(1)} %get-tuple-element.14), channel_id=1, source_target_pairs={{0,255},{1,16},{2,241},{3,18},{4,243},{5,20},{6,245},{7,22},{8,247... | collective-permute-start | bytes 6291464 | tf_op jit(solution)/shard_map/ppermute | solution.py:279
  117.7 4.9 %collective-permute-start.4 = (f32[8,16,1536]{2,1,0:T(8,128)S(1)}, f32[8,16,1536]{2,1,0:T(8,128)S(1)}, u32[]{:S(2)}, u32[]{:S(2)}) collective-permute-start(f32[8,16,1536]{2,1,0:T(8,128)S(1)} %slice_select_fusion), channel_id=1, source_target_pairs={{0,1},{1,0},{2,3},{3,2},{4,5},{5,4},{6,7},{7,6},{8,9},{9,8},{10,11... | collective-permute-start | bytes 2359304 | tf_op jit(solution)/shard_map/ppermute | solution.py:284

commit v3 on v2

--- a/solution.py
+++ b/solution.py
@@ -15,8 +15,20 @@
 BF = jnp.bfloat16
 F32 = jnp.float32
 MIB = 1024 * 1024
+SIDE = 4
 VMEM = pl.BlockSpec(memory_space=pltpu.VMEM)
 SMEM = pl.BlockSpec(memory_space=pltpu.SMEM)
+HBM = pl.BlockSpec(memory_space=pltpu.HBM)
+
+
+def snake(chip):
+    y, x = chip // SIDE, chip % SIDE
+    odd = y % 2
+    return y * SIDE + odd * (SIDE - 1 - x) + (1 - odd) * x
+
+
+def placed(q, count, odd):
+    return jnp.where(odd, snake(count - 1 - q), snake(q))
 
 
 def split(x):
@@ -36,18 +48,29 @@
     return pl.ds(pl.multiple_of(t * TILE, TILE), count * TILE)
 
 
-def send_kernel(core_ref, counts_ref, states_ref, weights_ref, scaled_ref, out_ref):
+def send_kernel(core_ref, counts_ref, states_hbm, weights_hbm, scaled_ref, out_ref, states_ref, weights_ref, sems):
     half = out_ref.shape[0]
-
-    @pl.loop(0, half * CHIP // 8)
-    def _(group):
-        for lane in range(8):
-            t = group * 8 + lane
-            count = jnp.full((1, TILE), counts_ref[t], jnp.int32).astype(F32)
-            scaled_ref[:, lanes(t)] = weights_ref[:, lanes(t)] * (count / (count + 8.0))
+    copies = [
+        pltpu.make_async_copy(source, target, sems.at[i])
+        for i, (source, target) in enumerate(((states_hbm, states_ref), (weights_hbm, weights_ref)))
+    ]
+    for copy in copies:
+        copy.start()
+
+    def scale():
+        @pl.loop(0, half * CHIP // 8)
+        def _(group):
+            for lane in range(8):
+                t = group * 8 + lane
+                count = jnp.full((1, TILE), counts_ref[t], jnp.int32).astype(F32)
+                scaled_ref[:, lanes(t)] = weights_ref[:, lanes(t)] * (count / (count + 8.0))
 
     rows = states_ref.shape[0]
+    copies[0].wait()
     for ref, there in ((states_ref, slice(0, rows)), (scaled_ref, slice(rows, None))):
+        if ref is scaled_ref:
+            copies[1].wait()
+            scale()
 
         @pl.when(core_ref[0] == 0)
         def _(ref=ref, there=there):
@@ -61,42 +84,48 @@
                 out_ref[q, there, cols(0, OWN)] = ref[:, cols(q * CHIP, OWN)]
 
 
-def merge_kernel(core_ref, states_ref, scaled_ref, got_ref, out_ref):
+def merge_kernel(core_ref, odd_ref, states_ref, scaled_ref, got_ref, out_ref):
     half = got_ref.shape[0]
     rows = states_ref.shape[0]
+    odd = odd_ref[0] != 0
 
     @pl.when(core_ref[0] == 0)
     def _():
         for q in range(half):
-            out_ref[q, :rows, :] = states_ref[:, cols(q * CHIP, OWN)]
-            out_ref[q, rows:, :] = scaled_ref[:, cols(q * CHIP, OWN)]
-            out_ref[half + q] = got_ref[q]
+            there = placed(q, 2 * half, odd)
+            out_ref[there, :rows, :] = states_ref[:, cols(q * CHIP, OWN)]
+            out_ref[there, rows:, :] = scaled_ref[:, cols(q * CHIP, OWN)]
+            out_ref[placed(half + q, 2 * half, odd)] = got_ref[q]
 
     @pl.when(core_ref[0] != 0)
     def _():
         for q in range(half):
+            there = placed(half + q, 2 * half, odd)
             for t in range(OWN):
-                out_ref[half + q, :rows, cols(t)] = states_ref[:, cols((q + 1) * CHIP - 1 - t)]
-                out_ref[half + q, rows:, cols(t)] = scaled_ref[:, cols((q + 1) * CHIP - 1 - t)]
-            out_ref[q] = got_ref[q]
-
-
-def place_kernel(core_ref, back_ref, got_ref, out_ref):
+                out_ref[there, :rows, cols(t)] = states_ref[:, cols((q + 1) * CHIP - 1 - t)]
+                out_ref[there, rows:, cols(t)] = scaled_ref[:, cols((q + 1) * CHIP - 1 - t)]
+            out_ref[placed(q, 2 * half, odd)] = got_ref[q]
+
+
+def place_kernel(core_ref, odd_ref, back_ref, got_ref, out_ref):
     half = got_ref.shape[0]
+    odd = odd_ref[0] != 0
 
     @pl.when(core_ref[0] == 0)
     def _():
         for q in range(half):
-            out_ref[:, cols(q * CHIP, OWN)] = back_ref[q]
+            there, theirs = placed(q, 2 * half, odd), placed(q, half, odd)
+            out_ref[:, cols(q * CHIP, OWN)] = back_ref[there]
             for t in range(OWN):
-                out_ref[:, cols((q + 1) * CHIP - 1 - t)] = got_ref[q, :, cols(t)]
+                out_ref[:, cols((q + 1) * CHIP - 1 - t)] = got_ref[theirs, :, cols(t)]
 
     @pl.when(core_ref[0] != 0)
     def _():
         for q in range(half):
-            out_ref[:, cols(q * CHIP, OWN)] = got_ref[q]
+            there, theirs = placed(half + q, 2 * half, odd), placed(q, half, odd)
+            out_ref[:, cols(q * CHIP, OWN)] = got_ref[theirs]
             for t in range(OWN):
-                out_ref[:, cols((q + 1) * CHIP - 1 - t)] = back_ref[half + q, :, cols(t)]
+                out_ref[:, cols((q + 1) * CHIP - 1 - t)] = back_ref[there, :, cols(t)]
 
 
 def anomaly_of(ref, t, members):
@@ -147,7 +176,7 @@
     return total[:members] + (total[members:] + dot(both[:members, band], low))
 
 
-def near_kernel(core_ref, mask_ref, mine_ref, other_ref, out_ref, ah, al, ath, atl, both, taper, ch, cl):
+def near_kernel(core_ref, mask_ref, mine_ref, other_ref, out_ref, ah, al, taper, ath, atl, both, ch, cl):
     members = ah.shape[0]
 
     @pl.loop(0, OWN)
@@ -167,39 +196,31 @@
         )
 
 
-def far_kernel(core_ref, mask_ref, mine_ref, halo_ref, near_ref, out_ref, ah, al, ath, atl, both, taper, ch, cl):
+def far_kernel(mask_ref, halo_ref, near_ref, ah, al, taper, out_ref, ath, atl, both, ch, cl):
     members = ah.shape[0]
 
     @pl.loop(0, HALO)
     def _(t):
         place_window(halo_ref, t, HALO - 1 - t, members, ath, atl, both)
-        place_own(mine_ref, t, members, ah, al)
-
-    place_taper(core_ref[0], HALO, taper)
-    for pair in range(PAIRS):
+
+    out_ref[:, cols(HALO, OWN - HALO)] = near_ref[:, cols(HALO, OWN - HALO)]
+    for pair in range(HALO // 2):
         there = cols(2 * pair, 2)
-        last = HALO - 2 * pair
-        if last > 0:
-            out_ref[:, there] = near_ref[:, there] + products(
-                pair, 0, last, 0, mask_ref, ah, al, ath, atl, both, taper, ch, cl
-            )
-        else:
-            out_ref[:, there] = near_ref[:, there]
-
-
-def windowed(kernel, members, own, window, span, flops, name):
+        out_ref[:, there] = near_ref[:, there] + products(
+            pair, 0, HALO - 2 * pair, 0, mask_ref, ah, al, ath, atl, both, taper, ch, cl
+        )
+
+
+def windowed(kernel, members, window, span, outs, ins, flops, name):
     return pl.pallas_call(
         kernel,
-        out_shape=jax.ShapeDtypeStruct((members, OWN * TILE), F32),
-        in_specs=[SMEM, VMEM, VMEM, VMEM] + [VMEM] * (name == "far"),
-        out_specs=VMEM,
+        out_shape=outs,
+        in_specs=ins,
+        out_specs=jax.tree.map(lambda _: VMEM, outs),
         scratch_shapes=[
-            pltpu.VMEM((members, own * TILE), BF),
-            pltpu.VMEM((members, own * TILE), BF),
             pltpu.VMEM((window * TILE, members), BF),
             pltpu.VMEM((window * TILE, members), BF),
             pltpu.VMEM((2 * members, window * TILE), BF),
-            pltpu.VMEM((span * TILE, 2 * TILE), F32),
             pltpu.VMEM((2, span * TILE, 2 * TILE), BF),
             pltpu.VMEM((2, span * TILE, 2 * TILE), BF),
         ],
@@ -209,13 +230,14 @@
     )
 
 
-def copying(kernel, outs, ins, name):
+def copying(kernel, outs, ins, name, scratch=(), limit=14):
     return pl.pallas_call(
         kernel,
         out_shape=outs,
         in_specs=ins,
         out_specs=jax.tree.map(lambda _: VMEM, outs),
-        compiler_params=pltpu.CompilerParams(vmem_limit_bytes=14 * MIB),
+        scratch_shapes=scratch,
+        compiler_params=pltpu.CompilerParams(vmem_limit_bytes=limit * MIB),
         cost_estimate=pl.CostEstimate(flops=0, bytes_accessed=6_000_000, transcendentals=0),
         name=name,
     )
@@ -239,12 +261,16 @@
 
 
 def outward(chips, regions):
+    def order(plane, place):
+        return snake(chips - 1 - place) if plane % 2 else snake(place)
+
     pairs = []
-    for chip in range(chips):
-        for region in range(regions):
-            plane, core = region // 2, region % 2
-            place = (plane * chips + chip + (1 if core else -1)) % (chips * regions // 2)
-            pairs.append((chip * regions + region, place % chips * regions + place // chips * 2 + 1 - core))
+    for plane in range(regions // 2):
+        for place in range(chips):
+            for core in range(2):
+                there, spot = divmod((plane * chips + place + (1 if core else -1)) % (chips * regions // 2), chips)
+                source = order(plane, place) * regions + plane * 2 + core
+                pairs.append((source, order(there, spot) * regions + there * 2 + 1 - core))
     return pairs
 
 
@@ -254,41 +280,65 @@
     rows, local = states.shape
     half = chips // 2
     core = lax.axis_index("region") % 2
-    chip = lax.axis_index("member")
+    odd = lax.axis_index("region") // 2 % 2
+    place = snake(lax.axis_index("member"))
+    chip = jnp.where(odd == 1, chips - 1 - place, place)
     swap = [(r, r ^ 1) for r in range(regions)]
     members = chips * rows
     flag = core.reshape(1)
+    flags = flag, odd.reshape(1)
     own = OWN * TILE
 
     scaled, sent = copying(
         send_kernel,
         (jax.ShapeDtypeStruct((rows, local), F32), jax.ShapeDtypeStruct((half, 2 * rows, own), F32)),
-        [SMEM, SMEM, VMEM, VMEM],
+        [SMEM, SMEM, HBM, HBM],
         "send",
+        [
+            pltpu.VMEM(states.shape, F32),
+            pltpu.VMEM(weights.shape, F32),
+            pltpu.SemaphoreType.DMA((2,)),
+        ],
+        limit=60,
     )(flag, obs_count, states, weights)
     got = lax.ppermute(sent, "region", swap)
     operand = copying(
         merge_kernel,
         jax.ShapeDtypeStruct((chips, 2 * rows, own), F32),
-        [SMEM, VMEM, VMEM, VMEM],
+        [SMEM, SMEM, VMEM, VMEM, VMEM],
         "merge",
-    )(flag, states, scaled, got)
+    )(*flags, states, scaled, got)
     mask = keep_mask(neighbours, core, chip, half, regions, 1.0 / (members - 1.0))
-    operand, mask = lax.optimization_barrier((operand, mask))
+    upper = core == odd
+    operand, mask, upper = lax.optimization_barrier((operand, mask, upper))
     mine = lax.all_to_all(operand, "member", split_axis=0, concat_axis=0, tiled=True)
     halo = lax.ppermute(mine[:, :, : HALO * TILE], ("member", "region"), outward(chips, regions))
     other = lax.ppermute(mine[:, :, own - HALO * TILE :], "region", swap)
-    near = windowed(near_kernel, members, OWN, OWN + HALO, SPAN, 18_000_000_000, "near")(flag, mask, mine, other)
-    total = windowed(far_kernel, members, HALO, HALO, HALO, 4_000_000_000, "far")(flag, mask, mine, halo, near)
+    total = jax.ShapeDtypeStruct((members, own), F32)
+    half_own = jax.ShapeDtypeStruct((members, own), BF)
+    tapers = jax.ShapeDtypeStruct((SPAN * TILE, 2 * TILE), F32)
+    near, high, low, tapers = windowed(
+        near_kernel,
+        members,
+        OWN + HALO,
+        SPAN,
+        (total, half_own, half_own, tapers),
+        [SMEM, VMEM, VMEM, VMEM],
+        18_000_000_000,
+        "near",
+    )(flag, mask, mine, other)
+    total = windowed(
+        far_kernel, members, HALO, HALO, total, [VMEM] * 6, 4_000_000_000, "far"
+    )(mask, halo, near, high, low, tapers)
     back = lax.all_to_all(total.reshape(chips, rows, own), "member", split_axis=0, concat_axis=0, tiled=True)
-    got = lax.ppermute(jnp.where(core == 0, back[half:], back[:half]), "region", swap)
+    got = lax.ppermute(jnp.where(upper, back[half:], back[:half]), "region", swap)
     return copying(
-        place_kernel, jax.ShapeDtypeStruct((rows, local), F32), [SMEM, VMEM, VMEM], "place"
-    )(flag, back, got)
+        place_kernel, jax.ShapeDtypeStruct((rows, local), F32), [SMEM, SMEM, VMEM, VMEM], "place"
+    )(*flags, back, got)
 
 
 def solution(mesh):
-    placed = (P("member", "region"), P("member", "region"), P("region"), P("region", None))
+    specs = (P("member", "region"), P("member", "region"), P("region"), P("region", None))
     return jax.shard_map(
-        shards, mesh=mesh, in_specs=placed, out_specs=P("member", "region"), check_vma=False
+        shards, mesh=mesh, in_specs=specs, out_specs=P("member", "region"), check_vma=False
     )

time: 125 us -> 119 us (0.952); the launches traced: 124 us -> 119 us
  blocking collectives: 71.2 us -> 65.7 us
  local copies, waits for them, and re-layouts: 4.48 us -> 2.39 us
  starting transfers between devices: 8.34 us -> 10.4 us
    all_to_all x1, blocking collectives: 27.2 us -> 21.6 us  [shards(): lax.all_to_all(total.reshape(chips, rows, own), 'member', split_axis=0, c...]
    pallas_call x1, Pallas kernels: 2.34 us -> 4.98 us  [shards(): copying(send_kernel, (jax.ShapeDtypeStruct((rows, local), F32), jax.Shape...]
    unnamed x12 -> x8, local copies, waits for them, and re-layouts: 3.55 us -> 1.46 us
    ppermute x1, starting transfers between devices: 2.99 us -> 4.9 us  [shards(): lax.ppermute(jnp.where(upper, back[half:], back[:half]), 'region', swap)]
    pallas_call x1, Pallas kernels: 1.62 us -> 0.22 us  [shards(): copying(merge_kernel, jax.ShapeDtypeStruct((chips, 2 * rows, own), F32),...]
  transfers between devices with their start and end apart: 5 -> 5, of which waited for: 4 -> 4; matrix products, arithmetic and copies ran while one was open for 1% -> 1% of each run, Pallas kernels for 11% -> 12%
where the time goes in v3:
time: 119 us
  blocking collectives  65.7 us (55%)
  Pallas kernels  24.6 us (21%)
  waiting for transfers between devices  15.5 us (13%)
  starting transfers between devices  10.4 us (9%)
  local copies, waits for them, and re-layouts  2.39 us (2%)
    all_to_all x1, blocking collectives, shards(): lax.all_to_all(operand, 'member', split_axis=0, concat_axis=0, tiled=True)  44 us
    all_to_all x1, blocking collectives, shards(): lax.all_to_all(total.reshape(chips, rows, own), 'member', split_axis=0, c...  21.6 us
    pallas_call x1, Pallas kernels, shards(): windowed(near_kernel, members, OWN + HALO, SPAN, (total, half_own, half_o...  14.4 us
    ppermute x1, waiting for transfers between devices, shards(): lax.ppermute(mine[:, :, :HALO * TILE], ('member', 'region'), outward(chip...  7.53 us
    pallas_call x1, Pallas kernels, shards(): copying(send_kernel, (jax.ShapeDtypeStruct((rows, local), F32), jax.Shape...  4.98 us
    ppermute x1, starting transfers between devices, shards(): lax.ppermute(jnp.where(upper, back[half:], back[:half]), 'region', swap)  4.9 us
    pallas_call x1, Pallas kernels, shards(): windowed(far_kernel, members, HALO, HALO, total, [VMEM] * 6, 4000000000,...  3.75 us
    ppermute x1, waiting for transfers between devices, shards(): other = lax.ppermute(mine[:, :, own - HALO * TILE:], 'region', swap)  3.34 us
  transfers between devices with their start and end apart: 5, of which 4 were waited for; matrix products, arithmetic and copies ran while one was open for 1% of the time, Pallas kernels for 12%

profile of v3, /device:TPU:1, one launch (start us, length us, event | category | flops | bytes accessed | tf_op | source)
XLA Modules:
  0.0 119.1 jit_solution(17000716651954712771)
XLA Ops:
  0.0 5.0 %send.1 = (f32[16,24576]{1,0:T(8,128)}, f32[8,32,1536]{2,1,0:T(8,128)}) custom-call(s32[1]{0:T(128)} %bitcast.core_ref, s32[192]{0:T(256)} %counts_ref.1, f32[16,24576]{1,0:T(8,128)} %states_ref.1, f32[16,24576]{1,0:T(8,128)} %weights_hbm.1), custom_call_target="tpu_custom_call" | custom-call | bytes 6000000 | tf_op jit(solution)/shard_map/send/pallas_call | solution.py:292
  5.0 3.3 %collective-permute-start = (f32[8,32,1536]{2,1,0:T(8,128)}, f32[8,32,1536]{2,1,0:T(8,128)S(1)}, u32[]{:S(2)}, u32[]{:S(2)}) collective-permute-start(f32[8,32,1536]{2,1,0:T(8,128)} %get-tuple-element.15), channel_id=1, source_target_pairs={{0,1},{1,0},{2,3},{3,2},{4,5},{5,4},{6,7},{7,6},{8,9},{9,8},{10,11... | collective-permute-start | bytes 4718600 | tf_op jit(solution)/shard_map/ppermute | solution.py:304
  8.3 0.1 collective-permute-start.1
  8.6 2.7 %collective-permute-done.1 = s32[192,12]{0,1:T(8,128)S(1)} collective-permute-done((s32[192,12]{0,1:T(8,128)S(1)}, s32[192,12]{0,1:T(8,128)S(1)}, u32[]{:S(2)}, u32[]{:S(2)}) %collective-permute-start.1) | collective-permute-done | bytes 9248 | tf_op jit(solution)/shard_map/ppermute | solution.py:247
  11.2 0.1 add_select_fusion
  11.4 0.1 copy.7
  11.5 0.1 compare_reduce_fusion
  11.7 0.1 copy.8
  11.8 0.2 broadcast_in_dim.14
  12.1 1.4 %copy-done.1 = f32[16,24576]{1,0:T(8,128)S(1)} copy-done((f32[16,24576]{1,0:T(8,128)S(1)}, f32[16,24576]{1,0:T(8,128)}, u32[]{:S(2)}) %copy-start.1) | copy-done | bytes 1572888
  13.5 0.2 merge.1
  13.7 44.0 %all_to_all.10.mine_ref = f32[16,32,1536]{2,1,0:T(8,128)S(1)} all-to-all(f32[16,32,1536]{2,1,0:T(8,128)S(1)} %merge.1), channel_id=1, replica_groups=mesh['member'=16,'region'=16] {'member'}, dimensions={0} | all-to-all | bytes 6291456 | tf_op jit(solution)/shard_map/all_to_all | solution.py:314
  57.7 0.4 fusion.3
  58.2 1.7 %collective-permute-start.3 = (f32[16,32,1024]{2,1,0:T(8,128)S(1)}, f32[16,32,1024]{2,1,0:T(8,128)S(1)}, u32[]{:S(2)}, u32[]{:S(2)}) collective-permute-start(f32[16,32,1024]{2,1,0:T(8,128)S(1)} %get-tuple-element.23), channel_id=1, source_target_pairs={{0,1},{1,0},{2,3},{3,2},{4,5},{5,4},{6,7},{7,6},{8,9},{9,8},{10,11... | collective-permute-start | bytes 6291464 | tf_op jit(solution)/shard_map/ppermute | solution.py:316
  59.8 0.5 collective-permute-start.2
  60.3 3.3 %collective-permute-done.3.other_ref = f32[16,32,1024]{2,1,0:T(8,128)S(1)} collective-permute-done((f32[16,32,1024]{2,1,0:T(8,128)S(1)}, f32[16,32,1024]{2,1,0:T(8,128)S(1)}, u32[]{:S(2)}, u32[]{:S(2)}) %collective-permute-start.3) | collective-permute-done | bytes 2097184 | tf_op jit(solution)/shard_map/ppermute | solution.py:316
  63.6 14.4 %near.1 = (f32[256,1536]{1,0:T(8,128)S(1)}, bf16[256,1536]{1,0:T(8,128)(2,1)S(1)}, bf16[256,1536]{1,0:T(8,128)(2,1)S(1)}, f32[2304,256]{1,0:T(8,128)S(1)}) custom-call(s32[1]{0:T(128)} %bitcast.core_ref, f32[108,256]{1,0:T(8,128)S(1)} %bitcast.10, f32[16,32,1536]{2,1,0:T(8,128)S(1)} %all_to_all.10.mine_ref, f32[16,32,1024]{2,1,0:T(8,128)S(1)} %collective-permute-done.3.other_ref), custom_call_target="tpu_custom_call" | custom-call | flops 17999998976 | bytes 8000000 | tf_op jit(solution)/shard_map/near/pallas_call | solution.py:320
  78.1 7.5 %collective-permute-done.2.halo_ref = f32[16,32,1024]{2,1,0:T(8,128)S(1)} collective-permute-done((f32[16,32,1024]{2,1,0:T(8,128)S(1)}, f32[16,32,1024]{2,1,0:T(8,128)S(1)}, u32[]{:S(2)}, u32[]{:S(2)}) %collective-permute-start.2) | collective-permute-done | bytes 2097184 | tf_op jit(solution)/shard_map/ppermute | solution.py:315
  85.6 3.8 %far.1 = f32[256,1536]{1,0:T(8,128)S(1)} custom-call(f32[108,256]{1,0:T(8,128)S(1)} %bitcast.11, f32[16,32,1024]{2,1,0:T(8,128)S(1)} %collective-permute-done.2.halo_ref, f32[256,1536]{1,0:T(8,128)S(1)} %get-tuple-element.18.near_ref, bf16[256,1536]{1,0:T(8,128)(2,1)S(1)} %get-tuple-element.19.ah, bf16[256,1536]{1,0:T(8,128)(2,1)S(1)} %get-tuple-element.20.al, ...), custom_call_target="tpu_custom_call" | custom-call | flops 4000000000 | bytes 8000000 | tf_op jit(solution)/shard_map/far/pallas_call | solution.py:330
  89.4 21.6 %all_to_all.11.back_ref = f32[16,16,1536]{2,1,0:T(8,128)S(1)} all-to-all(f32[16,16,1536]{2,1,0:T(8,128)S(1)} %bitcast.9), channel_id=1, replica_groups=mesh['member'=16,'region'=16] {'member'}, dimensions={0} | all-to-all | bytes 3145728 | tf_op jit(solution)/shard_map/all_to_all | solution.py:333
  111.0 0.1 slice_select_fusion
  111.1 4.9 %collective-permute-start.4 = (f32[8,16,1536]{2,1,0:T(8,128)S(1)}, f32[8,16,1536]{2,1,0:T(8,128)S(1)}, u32[]{:S(2)}, u32[]{:S(2)}) collective-permute-start(f32[8,16,1536]{2,1,0:T(8,128)S(1)} %slice_select_fusion), channel_id=1, source_target_pairs={{0,1},{1,0},{2,3},{3,2},{4,5},{5,4},{6,7},{7,6},{8,9},{9,8},{10,11... | collective-permute-start | bytes 2359304 | tf_op jit(solution)/shard_map/ppermute | solution.py:334
  116.0 1.9 %collective-permute-done.4.got_ref = f32[8,16,1536]{2,1,0:T(8,128)S(1)} collective-permute-done((f32[8,16,1536]{2,1,0:T(8,128)S(1)}, f32[8,16,1536]{2,1,0:T(8,128)S(1)}, u32[]{:S(2)}, u32[]{:S(2)}) %collective-permute-start.4) | collective-permute-done | bytes 786464 | tf_op jit(solution)/shard_map/ppermute | solution.py:334
  117.9 1.2 %place.1 = f32[16,24576]{1,0:T(8,128)} custom-call(s32[1]{0:T(128)} %bitcast.core_ref, s32[1]{0:T(128)} %bitcast.1.odd_ref, f32[16,16,1536]{2,1,0:T(8,128)S(1)} %all_to_all.11.back_ref, f32[8,16,1536]{2,1,0:T(8,128)S(1)} %collective-permute-done.4.got_ref), custom_call_target="tpu_custom_call" | custom-call | bytes 6000000 | tf_op jit(solution)/shard_map/place/pallas_call | solution.py:335
  (15 shorter events, 0.3 us)
Async XLA Ops:
  0.0 8.3 %copy-start.2 = (s32[192,12]{0,1:T(8,128)S(1)}, s32[192,12]{0,1:T(8,128)}, u32[]{:S(2)}) copy-start(s32[192,12]{0,1:T(8,128)} %param.7) | copy-start | bytes 27652
  0.0 12.1 %copy-start = (f32[16,24576]{1,0:T(8,128)S(1)}, f32[16,24576]{1,0:T(8,128)}, u32[]{:S(2)}) copy-start(f32[16,24576]{1,0:T(8,128)} %states_ref.1) | copy-start | bytes 4718596
  5.0 7.1 %collective-permute-start = (f32[8,32,1536]{2,1,0:T(8,128)}, f32[8,32,1536]{2,1,0:T(8,128)S(1)}, u32[]{:S(2)}, u32[]{:S(2)}) collective-permute-start(f32[8,32,1536]{2,1,0:T(8,128)} %get-tuple-element.15), channel_id=1, source_target_pairs={{0,1},{1,0},{2,3},{3,2},{4,5},{5,4},{6,7},{7,6},{8,9},{9,8},{10,11... | collective-permute-start | bytes 4718600 | tf_op jit(solution)/shard_map/ppermute | solution.py:304
  8.3 2.9 %collective-permute-start.1 = (s32[192,12]{0,1:T(8,128)S(1)}, s32[192,12]{0,1:T(8,128)S(1)}, u32[]{:S(2)}, u32[]{:S(2)}) collective-permute-start(s32[192,12]{0,1:T(8,128)S(1)} %copy-done.2), channel_id=1, source_target_pairs={{0,1},{1,0},{2,3},{3,2},{4,5},{5,4},{6,7},{7,6},{8,9},{9,8},{10,11... | collective-permute-start | bytes 27656 | tf_op jit(solution)/shard_map/ppermute | solution.py:247
  12.1 1.4 %copy-start.1 = (f32[16,24576]{1,0:T(8,128)S(1)}, f32[16,24576]{1,0:T(8,128)}, u32[]{:S(2)}) copy-start(f32[16,24576]{1,0:T(8,128)} %get-tuple-element.14.scaled_ref) | copy-start | bytes 4718596
  58.2 5.4 %collective-permute-start.3 = (f32[16,32,1024]{2,1,0:T(8,128)S(1)}, f32[16,32,1024]{2,1,0:T(8,128)S(1)}, u32[]{:S(2)}, u32[]{:S(2)}) collective-permute-start(f32[16,32,1024]{2,1,0:T(8,128)S(1)} %get-tuple-element.23), channel_id=1, source_target_pairs={{0,1},{1,0},{2,3},{3,2},{4,5},{5,4},{6,7},{7,6},{8,9},{9,8},{10,11... | collective-permute-start | bytes 6291464 | tf_op jit(solution)/shard_map/ppermute | solution.py:316
  59.8 25.8 %collective-permute-start.2 = (f32[16,32,1024]{2,1,0:T(8,128)S(1)}, f32[16,32,1024]{2,1,0:T(8,128)S(1)}, u32[]{:S(2)}, u32[]{:S(2)}) collective-permute-start(f32[16,32,1024]{2,1,0:T(8,128)S(1)} %get-tuple-element.24), channel_id=1, source_target_pairs={{0,15},{1,16},{16,1},{17,32},{32,17},{33,48},{48,33},{49,112},{112... | collective-permute-start | bytes 6291464 | tf_op jit(solution)/shard_map/ppermute | solution.py:315
  111.1 6.8 %collective-permute-start.4 = (f32[8,16,1536]{2,1,0:T(8,128)S(1)}, f32[8,16,1536]{2,1,0:T(8,128)S(1)}, u32[]{:S(2)}, u32[]{:S(2)}) collective-permute-start(f32[8,16,1536]{2,1,0:T(8,128)S(1)} %slice_select_fusion), channel_id=1, source_target_pairs={{0,1},{1,0},{2,3},{3,2},{4,5},{5,4},{6,7},{7,6},{8,9},{9,8},{10,11... | collective-permute-start | bytes 2359304 | tf_op jit(solution)/shard_map/ppermute | solution.py:334

commit v4 on v3

--- a/solution.py
+++ b/solution.py
@@ -48,29 +48,17 @@
     return pl.ds(pl.multiple_of(t * TILE, TILE), count * TILE)
 
 
-def send_kernel(core_ref, counts_ref, states_hbm, weights_hbm, scaled_ref, out_ref, states_ref, weights_ref, sems):
+def send_kernel(core_ref, states_hbm, weights_hbm, out_ref, states_ref, weights_ref, sems):
     half = out_ref.shape[0]
-    copies = [
-        pltpu.make_async_copy(source, target, sems.at[i])
-        for i, (source, target) in enumerate(((states_hbm, states_ref), (weights_hbm, weights_ref)))
-    ]
-    for copy in copies:
+    rows = states_ref.shape[0]
+    parts = (
+        (pltpu.make_async_copy(states_hbm, states_ref, sems.at[0]), states_ref, slice(0, rows)),
+        (pltpu.make_async_copy(weights_hbm, weights_ref, sems.at[1]), weights_ref, slice(rows, None)),
+    )
+    for copy, _, _ in parts:
         copy.start()
-
-    def scale():
-        @pl.loop(0, half * CHIP // 8)
-        def _(group):
-            for lane in range(8):
-                t = group * 8 + lane
-                count = jnp.full((1, TILE), counts_ref[t], jnp.int32).astype(F32)
-                scaled_ref[:, lanes(t)] = weights_ref[:, lanes(t)] * (count / (count + 8.0))
-
-    rows = states_ref.shape[0]
-    copies[0].wait()
-    for ref, there in ((states_ref, slice(0, rows)), (scaled_ref, slice(rows, None))):
-        if ref is scaled_ref:
-            copies[1].wait()
-            scale()
+    for copy, ref, there in parts:
+        copy.wait()
 
         @pl.when(core_ref[0] == 0)
         def _(ref=ref, there=there):
@@ -84,7 +72,13 @@
                 out_ref[q, there, cols(0, OWN)] = ref[:, cols(q * CHIP, OWN)]
 
 
-def merge_kernel(core_ref, odd_ref, states_ref, scaled_ref, got_ref, out_ref):
+def scale(ref, q, rows, counts_ref, first, step):
+    for t in range(OWN):
+        count = jnp.full((1, TILE), counts_ref[first + step * t], jnp.int32).astype(F32)
+        ref[q, rows:, cols(t)] = ref[q, rows:, cols(t)] * (count / (count + 8.0))
+
+
+def merge_kernel(core_ref, odd_ref, counts_ref, theirs_ref, states_ref, weights_ref, got_ref, out_ref):
     half = got_ref.shape[0]
     rows = states_ref.shape[0]
     odd = odd_ref[0] != 0
@@ -94,8 +88,11 @@
         for q in range(half):
             there = placed(q, 2 * half, odd)
             out_ref[there, :rows, :] = states_ref[:, cols(q * CHIP, OWN)]
-            out_ref[there, rows:, :] = scaled_ref[:, cols(q * CHIP, OWN)]
-            out_ref[placed(half + q, 2 * half, odd)] = got_ref[q]
+            out_ref[there, rows:, :] = weights_ref[:, cols(q * CHIP, OWN)]
+            scale(out_ref, there, rows, counts_ref, q * CHIP, 1)
+            there = placed(half + q, 2 * half, odd)
+            out_ref[there] = got_ref[q]
+            scale(out_ref, there, rows, theirs_ref, q * CHIP, 1)
 
     @pl.when(core_ref[0] != 0)
     def _():
@@ -103,8 +100,11 @@
             there = placed(half + q, 2 * half, odd)
             for t in range(OWN):
                 out_ref[there, :rows, cols(t)] = states_ref[:, cols((q + 1) * CHIP - 1 - t)]
-                out_ref[there, rows:, cols(t)] = scaled_ref[:, cols((q + 1) * CHIP - 1 - t)]
-            out_ref[placed(q, 2 * half, odd)] = got_ref[q]
+                out_ref[there, rows:, cols(t)] = weights_ref[:, cols((q + 1) * CHIP - 1 - t)]
+            scale(out_ref, there, rows, counts_ref, (q + 1) * CHIP - 1, -1)
+            there = placed(q, 2 * half, odd)
+            out_ref[there] = got_ref[q]
+            scale(out_ref, there, rows, theirs_ref, (q + 1) * CHIP - 1, -1)
 
 
 def place_kernel(core_ref, odd_ref, back_ref, got_ref, out_ref):
@@ -289,25 +289,22 @@
     flags = flag, odd.reshape(1)
     own = OWN * TILE
 
-    scaled, sent = copying(
+    sent = copying(
         send_kernel,
-        (jax.ShapeDtypeStruct((rows, local), F32), jax.ShapeDtypeStruct((half, 2 * rows, own), F32)),
-        [SMEM, SMEM, HBM, HBM],
+        jax.ShapeDtypeStruct((half, 2 * rows, own), F32),
+        [SMEM, HBM, HBM],
         "send",
-        [
-            pltpu.VMEM(states.shape, F32),
-            pltpu.VMEM(weights.shape, F32),
-            pltpu.SemaphoreType.DMA((2,)),
-        ],
+        [pltpu.VMEM(states.shape, F32), pltpu.VMEM(weights.shape, F32), pltpu.SemaphoreType.DMA((2,))],
         limit=60,
-    )(flag, obs_count, states, weights)
+    )(flag, states, weights)
+    sent, obs_count, neighbours = lax.optimization_barrier((sent, obs_count, neighbours))
     got = lax.ppermute(sent, "region", swap)
     operand = copying(
         merge_kernel,
         jax.ShapeDtypeStruct((chips, 2 * rows, own), F32),
-        [SMEM, SMEM, VMEM, VMEM, VMEM],
+        [SMEM] * 4 + [VMEM] * 3,
         "merge",
-    )(*flags, states, scaled, got)
+    )(*flags, obs_count, lax.ppermute(obs_count, "region", swap), states, weights, got)
     mask = keep_mask(neighbours, core, chip, half, regions, 1.0 / (members - 1.0))
     upper = core == odd
     operand, mask, upper = lax.optimization_barrier((operand, mask, upper))

time: 119 us -> 118 us (level)
  local copies, waits for them, and re-layouts: 2.39 us -> 1 us
    pallas_call x1, Pallas kernels: 4.98 us -> 3.24 us  [shards(): copying(send_kernel, jax.ShapeDtypeStruct((half, 2 * rows, own), F32), [S...]
    pallas_call x1, Pallas kernels: 0.22 us -> 1.68 us  [shards(): copying(merge_kernel, jax.ShapeDtypeStruct((chips, 2 * rows, own), F32),...]
    unnamed x8 -> x10, local copies, waits for them, and re-layouts: 1.46 us -> 0.07 us
  transfers between devices with their start and end apart: 5 -> 6, of which waited for: 4 -> 4; matrix products, arithmetic and copies ran while one was open for 1% -> 1% of each run, Pallas kernels for 12% -> 12%
where the time goes in v4:
time: 118 us; the launch traced here: 117 us
  blocking collectives  65.3 us (55%)
  Pallas kernels  24.3 us (21%)
  waiting for transfers between devices  15.3 us (13%)
  starting transfers between devices  11 us (9%)
    all_to_all x1, blocking collectives, shards(): lax.all_to_all(operand, 'member', split_axis=0, concat_axis=0, tiled=True)  43.6 us
    all_to_all x1, blocking collectives, shards(): lax.all_to_all(total.reshape(chips, rows, own), 'member', split_axis=0, c...  21.6 us
    pallas_call x1, Pallas kernels, shards(): windowed(near_kernel, members, OWN + HALO, SPAN, (total, half_own, half_o...  14.3 us
    ppermute x1, waiting for transfers between devices, shards(): lax.ppermute(mine[:, :, :HALO * TILE], ('member', 'region'), outward(chip...  7.62 us
    ppermute x1, starting transfers between devices, shards(): lax.ppermute(jnp.where(upper, back[half:], back[:half]), 'region', swap)  4.9 us
    pallas_call x1, Pallas kernels, shards(): windowed(far_kernel, members, HALO, HALO, total, [VMEM] * 6, 4000000000,...  3.74 us
    ppermute x1, waiting for transfers between devices, shards(): other = lax.ppermute(mine[:, :, own - HALO * TILE:], 'region', swap)  3.34 us
    ppermute x1, starting transfers between devices, shards(): got = lax.ppermute(sent, 'region', swap)  3.32 us
  transfers between devices with their start and end apart: 6, of which 4 were waited for; matrix products, arithmetic and copies ran while one was open for 1% of the time, Pallas kernels for 12%

profile of v4, /device:TPU:1, one launch (start us, length us, event | category | flops | bytes accessed | tf_op | source)
XLA Modules:
  0.0 117.4 jit_solution(17676054850981871676)
XLA Ops:
  0.0 3.2 %send.1 = f32[8,32,1536]{2,1,0:T(8,128)} custom-call(s32[1]{0:T(128)} %bitcast.core_ref, f32[16,24576]{1,0:T(8,128)} %states_ref.1, f32[16,24576]{1,0:T(8,128)} %weights_ref.1), custom_call_target="tpu_custom_call" | custom-call | bytes 6000000 | tf_op jit(solution)/shard_map/send/pallas_call | solution.py:292
  3.3 3.3 %collective-permute-start.1 = (f32[8,32,1536]{2,1,0:T(8,128)}, f32[8,32,1536]{2,1,0:T(8,128)}, u32[]{:S(2)}, u32[]{:S(2)}) collective-permute-start(f32[8,32,1536]{2,1,0:T(8,128)} %send.1), channel_id=1, source_target_pairs={{0,1},{1,0},{2,3},{3,2},{4,5},{5,4},{6,7},{7,6},{8,9},{9,8},{10,11... | collective-permute-start | bytes 4718600 | tf_op jit(solution)/shard_map/ppermute | solution.py:301
  6.6 0.1 collective-permute-start
  6.7 0.4 collective-permute-start.2
  7.2 2.4 %collective-permute-done.2 = s32[192,12]{0,1:T(8,128)S(1)} collective-permute-done((s32[192,12]{0,1:T(8,128)S(1)}, s32[192,12]{0,1:T(8,128)S(1)}, u32[]{:S(2)}, u32[]{:S(2)}) %collective-permute-start.2) | collective-permute-done | bytes 9248 | tf_op jit(solution)/shard_map/ppermute | solution.py:247
  9.7 0.1 add_select_fusion
  9.8 0.1 copy.7
  9.9 0.1 compare_reduce_fusion
  10.1 0.1 copy.8
  10.2 0.2 broadcast_in_dim.14
  10.5 1.7 %merge.1 = f32[16,32,1536]{2,1,0:T(8,128)S(1)} custom-call(s32[1]{0:T(128)} %bitcast.core_ref, s32[1]{0:T(128)} %bitcast.1.odd_ref, s32[192]{0:T(256)S(1)} %copy-done.2, s32[192]{0:T(256)S(1)} %collective-permute-done.theirs_ref, f32[16,24576]{1,0:T(8,128)S(1)} %copy-done, f32[16,24576]{1,0:T(8,128)S(1)} %copy-done.1, ...), custom_call_target="tpu_custom_call" | custom-call | bytes 6000000 | tf_op jit(solution)/shard_map/merge/pallas_call | solution.py:302
  12.2 43.6 %all_to_all.10.mine_ref = f32[16,32,1536]{2,1,0:T(8,128)S(1)} all-to-all(f32[16,32,1536]{2,1,0:T(8,128)S(1)} %merge.1), channel_id=1, replica_groups=mesh['member'=16,'region'=16] {'member'}, dimensions={0} | all-to-all | bytes 6291456 | tf_op jit(solution)/shard_map/all_to_all | solution.py:311
  55.8 0.4 fusion.3
  56.2 1.9 %collective-permute-start.4 = (f32[16,32,1024]{2,1,0:T(8,128)S(1)}, f32[16,32,1024]{2,1,0:T(8,128)S(1)}, u32[]{:S(2)}, u32[]{:S(2)}) collective-permute-start(f32[16,32,1024]{2,1,0:T(8,128)S(1)} %get-tuple-element.25), channel_id=1, source_target_pairs={{0,1},{1,0},{2,3},{3,2},{4,5},{5,4},{6,7},{7,6},{8,9},{9,8},{10,11... | collective-permute-start | bytes 6291464 | tf_op jit(solution)/shard_map/ppermute | solution.py:313
  58.1 0.5 collective-permute-start.3
  58.6 3.3 %collective-permute-done.4.other_ref = f32[16,32,1024]{2,1,0:T(8,128)S(1)} collective-permute-done((f32[16,32,1024]{2,1,0:T(8,128)S(1)}, f32[16,32,1024]{2,1,0:T(8,128)S(1)}, u32[]{:S(2)}, u32[]{:S(2)}) %collective-permute-start.4) | collective-permute-done | bytes 2097184 | tf_op jit(solution)/shard_map/ppermute | solution.py:313
  61.9 14.3 %near.1 = (f32[256,1536]{1,0:T(8,128)S(1)}, bf16[256,1536]{1,0:T(8,128)(2,1)S(1)}, bf16[256,1536]{1,0:T(8,128)(2,1)S(1)}, f32[2304,256]{1,0:T(8,128)S(1)}) custom-call(s32[1]{0:T(128)} %bitcast.core_ref, f32[108,256]{1,0:T(8,128)S(1)} %bitcast.10, f32[16,32,1536]{2,1,0:T(8,128)S(1)} %all_to_all.10.mine_ref, f32[16,32,1024]{2,1,0:T(8,128)S(1)} %collective-permute-done.4.other_ref), custom_call_target="tpu_custom_call" | custom-call | flops 17999998976 | bytes 8000000 | tf_op jit(solution)/shard_map/near/pallas_call | solution.py:317
  76.3 7.6 %collective-permute-done.3.halo_ref = f32[16,32,1024]{2,1,0:T(8,128)S(1)} collective-permute-done((f32[16,32,1024]{2,1,0:T(8,128)S(1)}, f32[16,32,1024]{2,1,0:T(8,128)S(1)}, u32[]{:S(2)}, u32[]{:S(2)}) %collective-permute-start.3) | collective-permute-done | bytes 2097184 | tf_op jit(solution)/shard_map/ppermute | solution.py:312
  83.9 3.7 %far.1 = f32[256,1536]{1,0:T(8,128)S(1)} custom-call(f32[108,256]{1,0:T(8,128)S(1)} %bitcast.11, f32[16,32,1024]{2,1,0:T(8,128)S(1)} %collective-permute-done.3.halo_ref, f32[256,1536]{1,0:T(8,128)S(1)} %get-tuple-element.20.near_ref, bf16[256,1536]{1,0:T(8,128)(2,1)S(1)} %get-tuple-element.21.ah, bf16[256,1536]{1,0:T(8,128)(2,1)S(1)} %get-tuple-element.22.al, ...), custom_call_target="tpu_custom_call" | custom-call | flops 4000000000 | bytes 8000000 | tf_op jit(solution)/shard_map/far/pallas_call | solution.py:327
  87.6 21.6 %all_to_all.11.back_ref = f32[16,16,1536]{2,1,0:T(8,128)S(1)} all-to-all(f32[16,16,1536]{2,1,0:T(8,128)S(1)} %bitcast.9), channel_id=1, replica_groups=mesh['member'=16,'region'=16] {'member'}, dimensions={0} | all-to-all | bytes 3145728 | tf_op jit(solution)/shard_map/all_to_all | solution.py:330
  109.2 0.1 slice_select_fusion
  109.3 4.9 %collective-permute-start.5 = (f32[8,16,1536]{2,1,0:T(8,128)S(1)}, f32[8,16,1536]{2,1,0:T(8,128)S(1)}, u32[]{:S(2)}, u32[]{:S(2)}) collective-permute-start(f32[8,16,1536]{2,1,0:T(8,128)S(1)} %slice_select_fusion), channel_id=1, source_target_pairs={{0,1},{1,0},{2,3},{3,2},{4,5},{5,4},{6,7},{7,6},{8,9},{9,8},{10,11... | collective-permute-start | bytes 2359304 | tf_op jit(solution)/shard_map/ppermute | solution.py:331
  114.2 1.9 %collective-permute-done.5.got_ref = f32[8,16,1536]{2,1,0:T(8,128)S(1)} collective-permute-done((f32[8,16,1536]{2,1,0:T(8,128)S(1)}, f32[8,16,1536]{2,1,0:T(8,128)S(1)}, u32[]{:S(2)}, u32[]{:S(2)}) %collective-permute-start.5) | collective-permute-done | bytes 786464 | tf_op jit(solution)/shard_map/ppermute | solution.py:331
  116.2 1.2 %place.1 = f32[16,24576]{1,0:T(8,128)} custom-call(s32[1]{0:T(128)} %bitcast.core_ref, s32[1]{0:T(128)} %bitcast.1.odd_ref, f32[16,16,1536]{2,1,0:T(8,128)S(1)} %all_to_all.11.back_ref, f32[8,16,1536]{2,1,0:T(8,128)S(1)} %collective-permute-done.5.got_ref), custom_call_target="tpu_custom_call" | custom-call | bytes 6000000 | tf_op jit(solution)/shard_map/place/pallas_call | solution.py:332
  (19 shorter events, 0.3 us)
Async XLA Ops:
  0.0 6.6 %copy-start.2 = (s32[192]{0:T(256)S(1)}, s32[192]{0:T(256)}, u32[]{:S(2)}) copy-start(s32[192]{0:T(256)} %counts_ref) | copy-start | bytes 2308
  0.0 6.7 %copy-start.3 = (s32[192,12]{0,1:T(8,128)S(1)}, s32[192,12]{0,1:T(8,128)}, u32[]{:S(2)}) copy-start(s32[192,12]{0,1:T(8,128)} %param.7) | copy-start | bytes 27652
  0.0 10.5 %copy-start = (f32[16,24576]{1,0:T(8,128)S(1)}, f32[16,24576]{1,0:T(8,128)}, u32[]{:S(2)}) copy-start(f32[16,24576]{1,0:T(8,128)} %states_ref.1) | copy-start | bytes 4718596
  0.0 10.5 %copy-start.1 = (f32[16,24576]{1,0:T(8,128)S(1)}, f32[16,24576]{1,0:T(8,128)}, u32[]{:S(2)}) copy-start(f32[16,24576]{1,0:T(8,128)} %weights_ref.1) | copy-start | bytes 4718596
  3.3 7.2 %collective-permute-start.1 = (f32[8,32,1536]{2,1,0:T(8,128)}, f32[8,32,1536]{2,1,0:T(8,128)}, u32[]{:S(2)}, u32[]{:S(2)}) collective-permute-start(f32[8,32,1536]{2,1,0:T(8,128)} %send.1), channel_id=1, source_target_pairs={{0,1},{1,0},{2,3},{3,2},{4,5},{5,4},{6,7},{7,6},{8,9},{9,8},{10,11... | collective-permute-start | bytes 4718600 | tf_op jit(solution)/shard_map/ppermute | solution.py:301
  6.6 3.9 %collective-permute-start = (s32[192]{0:T(256)S(1)}, s32[192]{0:T(256)S(1)}, u32[]{:S(2)}, u32[]{:S(2)}) collective-permute-start(s32[192]{0:T(256)S(1)} %copy-done.2), channel_id=1, source_target_pairs={{0,1},{1,0},{2,3},{3,2},{4,5},{5,4},{6,7},{7,6},{8,9},{9,8},{10,11... | collective-permute-start | bytes 2312 | tf_op jit(solution)/shard_map/ppermute | solution.py:307
  6.7 2.9 %collective-permute-start.2 = (s32[192,12]{0,1:T(8,128)S(1)}, s32[192,12]{0,1:T(8,128)S(1)}, u32[]{:S(2)}, u32[]{:S(2)}) collective-permute-start(s32[192,12]{0,1:T(8,128)S(1)} %copy-done.3), channel_id=1, source_target_pairs={{0,1},{1,0},{2,3},{3,2},{4,5},{5,4},{6,7},{7,6},{8,9},{9,8},{10,11... | collective-permute-start | bytes 27656 | tf_op jit(solution)/shard_map/ppermute | solution.py:247
  56.2 5.7 %collective-permute-start.4 = (f32[16,32,1024]{2,1,0:T(8,128)S(1)}, f32[16,32,1024]{2,1,0:T(8,128)S(1)}, u32[]{:S(2)}, u32[]{:S(2)}) collective-permute-start(f32[16,32,1024]{2,1,0:T(8,128)S(1)} %get-tuple-element.25), channel_id=1, source_target_pairs={{0,1},{1,0},{2,3},{3,2},{4,5},{5,4},{6,7},{7,6},{8,9},{9,8},{10,11... | collective-permute-start | bytes 6291464 | tf_op jit(solution)/shard_map/ppermute | solution.py:313
  58.1 25.8 %collective-permute-start.3 = (f32[16,32,1024]{2,1,0:T(8,128)S(1)}, f32[16,32,1024]{2,1,0:T(8,128)S(1)}, u32[]{:S(2)}, u32[]{:S(2)}) collective-permute-start(f32[16,32,1024]{2,1,0:T(8,128)S(1)} %get-tuple-element.26), channel_id=1, source_target_pairs={{0,15},{1,16},{16,1},{17,32},{32,17},{33,48},{48,33},{49,112},{112... | collective-permute-start | bytes 6291464 | tf_op jit(solution)/shard_map/ppermute | solution.py:312
  109.3 6.8 %collective-permute-start.5 = (f32[8,16,1536]{2,1,0:T(8,128)S(1)}, f32[8,16,1536]{2,1,0:T(8,128)S(1)}, u32[]{:S(2)}, u32[]{:S(2)}) collective-permute-start(f32[8,16,1536]{2,1,0:T(8,128)S(1)} %slice_select_fusion), channel_id=1, source_target_pairs={{0,1},{1,0},{2,3},{3,2},{4,5},{5,4},{6,7},{7,6},{8,9},{9,8},{10,11... | collective-permute-start | bytes 2359304 | tf_op jit(solution)/shard_map/ppermute | solution.py:331

commit v5 on v4

--- a/solution.py
+++ b/solution.py
@@ -134,9 +134,13 @@
     return state - jnp.sum(state, axis=0, keepdims=True) * (1.0 / members)
 
 
-def place_window(ref, t, w, members, ath, atl, both):
+def place_anomaly(ref, t, w, members, ath, atl):
     ath[lanes(w), :], atl[lanes(w), :] = split(anomaly_of(ref, t, members).T)
-    weights = ref[:, members // ref.shape[0] :, lanes(t)].reshape(members, TILE)
+
+
+def place_weights(ref, t, w, members, both):
+    rows = members // ref.shape[0]
+    weights = ref[:, ref.shape[1] - rows :, lanes(t)].reshape(members, TILE)
     both[:members, lanes(w)], both[members:, lanes(w)] = split(weights)
 
 
@@ -157,10 +161,8 @@
         taper[lanes(k), :] = 1.0 / (1.0 + scaled * scaled)
 
 
-def products(pair, first, last, skip, mask_ref, ah, al, ath, atl, both, taper, ch, cl):
-    members = ah.shape[0]
+def coefficients(pair, first, last, skip, mask_ref, ah, al, ath, atl, taper, ch, cl, base):
     own_high, own_low = ah[:, cols(2 * pair, 2)], al[:, cols(2 * pair, 2)]
-    slot = pair % 2
     for k in range(first, last, 2):
         there = cols(2 * pair + k - skip, 2)
         high = ath[there, :]
@@ -168,12 +170,16 @@
         covar = covar * taper[cols(k, 2), :]
         for half in range(2):
             keep = mask_ref[pair * SPAN + k + half : pair * SPAN + k + half + 1, :]
-            coefficient = covar[half * TILE : (half + 1) * TILE] * keep
-            ch[slot, cols(k + half), :], cl[slot, cols(k + half), :] = split(coefficient)
+            spot = cols(base + k + half)
+            ch[spot, :], cl[spot, :] = split(covar[half * TILE : (half + 1) * TILE] * keep)
+
+
+def applied(pair, first, last, skip, both, ch, cl, base):
+    members = both.shape[0] // 2
     band = cols(2 * pair + first - skip, last - first)
-    high, low = ch[slot, cols(first, last - first), :], cl[slot, cols(first, last - first), :]
-    total = dot(both[:, band], high)
-    return total[:members] + (total[members:] + dot(both[:members, band], low))
+    there = cols(base + first, last - first)
+    total = dot(both[:, band], ch[there, :])
+    return total[:members] + (total[members:] + dot(both[:members, band], cl[there, :]))
 
 
 def near_kernel(core_ref, mask_ref, mine_ref, other_ref, out_ref, ah, al, taper, ath, atl, both, ch, cl):
@@ -181,49 +187,53 @@
 
     @pl.loop(0, OWN)
     def _(t):
-        place_window(mine_ref, t, t, members, ath, atl, both)
+        place_anomaly(mine_ref, t, t, members, ath, atl)
+        place_weights(mine_ref, t, t, members, both)
         place_own(mine_ref, t, members, ah, al)
 
     @pl.loop(0, HALO)
     def _(t):
-        place_window(other_ref, t, OWN + HALO - 1 - t, members, ath, atl, both)
+        place_anomaly(other_ref, t, OWN + HALO - 1 - t, members, ath, atl)
+        place_weights(other_ref, t, OWN + HALO - 1 - t, members, both)
 
     place_taper(core_ref[0], SPAN, taper)
     for pair in range(PAIRS):
-        first = max(0, HALO - 2 * pair)
-        out_ref[:, cols(2 * pair, 2)] = products(
-            pair, first, SPAN, HALO, mask_ref, ah, al, ath, atl, both, taper, ch, cl
-        )
-
-
-def far_kernel(mask_ref, halo_ref, near_ref, ah, al, taper, out_ref, ath, atl, both, ch, cl):
+        first, base = max(0, HALO - 2 * pair), pair % 2 * SPAN
+        coefficients(pair, first, SPAN, HALO, mask_ref, ah, al, ath, atl, taper, ch, cl, base)
+        out_ref[:, cols(2 * pair, 2)] = applied(pair, first, SPAN, HALO, both, ch, cl, base)
+
+
+def far_kernel(mask_ref, halo_ref, ah, al, taper, ch, cl, ath, atl):
     members = ah.shape[0]
 
     @pl.loop(0, HALO)
     def _(t):
-        place_window(halo_ref, t, HALO - 1 - t, members, ath, atl, both)
+        place_anomaly(halo_ref, t, HALO - 1 - t, members, ath, atl)
+
+    for pair in range(HALO // 2):
+        coefficients(pair, 0, HALO - 2 * pair, 0, mask_ref, ah, al, ath, atl, taper, ch, cl, pair * HALO)
+
+
+def add_kernel(halo_ref, near_ref, ch, cl, out_ref, both):
+    members = out_ref.shape[0]
+
+    @pl.loop(0, HALO)
+    def _(t):
+        place_weights(halo_ref, t, HALO - 1 - t, members, both)
 
     out_ref[:, cols(HALO, OWN - HALO)] = near_ref[:, cols(HALO, OWN - HALO)]
     for pair in range(HALO // 2):
         there = cols(2 * pair, 2)
-        out_ref[:, there] = near_ref[:, there] + products(
-            pair, 0, HALO - 2 * pair, 0, mask_ref, ah, al, ath, atl, both, taper, ch, cl
-        )
-
-
-def windowed(kernel, members, window, span, outs, ins, flops, name):
+        out_ref[:, there] = near_ref[:, there] + applied(pair, 0, HALO - 2 * pair, 0, both, ch, cl, pair * HALO)
+
+
+def windowed(kernel, outs, ins, scratch, flops, name):
     return pl.pallas_call(
         kernel,
         out_shape=outs,
         in_specs=ins,
         out_specs=jax.tree.map(lambda _: VMEM, outs),
-        scratch_shapes=[
-            pltpu.VMEM((window * TILE, members), BF),
-            pltpu.VMEM((window * TILE, members), BF),
-            pltpu.VMEM((2 * members, window * TILE), BF),
-            pltpu.VMEM((2, span * TILE, 2 * TILE), BF),
-            pltpu.VMEM((2, span * TILE, 2 * TILE), BF),
-        ],
+        scratch_shapes=[pltpu.VMEM(shape, BF) for shape in scratch],
         compiler_params=pltpu.CompilerParams(vmem_limit_bytes=32 * MIB),
         cost_estimate=pl.CostEstimate(flops=flops, bytes_accessed=8_000_000, transcendentals=0),
         name=name,
@@ -309,24 +319,34 @@
     upper = core == odd
     operand, mask, upper = lax.optimization_barrier((operand, mask, upper))
     mine = lax.all_to_all(operand, "member", split_axis=0, concat_axis=0, tiled=True)
-    halo = lax.ppermute(mine[:, :, : HALO * TILE], ("member", "region"), outward(chips, regions))
+    axes, out = ("member", "region"), outward(chips, regions)
+    halo = lax.ppermute(mine[:, :rows, : HALO * TILE], axes, out)
+    halo_weights = lax.ppermute(mine[:, rows:, : HALO * TILE], axes, out)
     other = lax.ppermute(mine[:, :, own - HALO * TILE :], "region", swap)
     total = jax.ShapeDtypeStruct((members, own), F32)
     half_own = jax.ShapeDtypeStruct((members, own), BF)
     tapers = jax.ShapeDtypeStruct((SPAN * TILE, 2 * TILE), F32)
+    window = (OWN + HALO) * TILE
     near, high, low, tapers = windowed(
         near_kernel,
-        members,
-        OWN + HALO,
-        SPAN,
         (total, half_own, half_own, tapers),
         [SMEM, VMEM, VMEM, VMEM],
+        [(window, members)] * 2 + [(2 * members, window)] + [(2 * SPAN * TILE, 2 * TILE)] * 2,
         18_000_000_000,
         "near",
     )(flag, mask, mine, other)
+    coefficient = jax.ShapeDtypeStruct((HALO // 2 * HALO * TILE, 2 * TILE), BF)
+    high, low = windowed(
+        far_kernel,
+        (coefficient, coefficient),
+        [VMEM] * 5,
+        [(HALO * TILE, members)] * 2,
+        2_000_000_000,
+        "far",
+    )(mask, halo, high, low, tapers)
     total = windowed(
-        far_kernel, members, HALO, HALO, total, [VMEM] * 6, 4_000_000_000, "far"
-    )(mask, halo, near, high, low, tapers)
+        add_kernel, total, [VMEM] * 4, [(2 * members, HALO * TILE)], 2_000_000_000, "add"
+    )(halo_weights, near, high, low)
     back = lax.all_to_all(total.reshape(chips, rows, own), "member", split_axis=0, concat_axis=0, tiled=True)
     got = lax.ppermute(jnp.where(upper, back[half:], back[:half]), "region", swap)
     return copying(

time: 118 us -> 115 us (0.975)
  waiting for transfers between devices: 15.3 us -> 11.4 us
  starting transfers between devices: 11 us -> 12.2 us
    ppermute x1 -> x2, waiting for transfers between devices: 7.62 us -> 5.45 us  [the longest x1 5.45 us: shards(): halo_weights = lax.ppermute(mine[:, rows:, :HALO * TILE], axes, out)]
    ppermute x1, waiting for transfers between devices: 3.34 us -> 1.77 us  [shards(): other = lax.ppermute(mine[:, :, own - HALO * TILE:], 'region', swap)]
    ppermute x1 -> x2, starting transfers between devices: 0.45 us -> 1.83 us  [the longest x1 1.56 us: shards(): halo_weights = lax.ppermute(mine[:, rows:, :HALO * TILE], axes, out)]
    pallas_call x2 -> x3, Pallas kernels: 18.1 us -> 18.3 us  [the longest x1 14.3 us: shards(): windowed(near_kernel, (total, half_own, half_own, tapers), [SMEM, VMEM, V...]
  transfers between devices with their start and end apart: 6 -> 7, of which waited for: 4 -> 4; matrix products, arithmetic and copies ran while one was open for 1% -> 1% of each run, Pallas kernels for 12% -> 15%
where the time goes in v5:
time: 115 us
  blocking collectives  65.7 us (57%)
  Pallas kernels  24.5 us (21%)
  starting transfers between devices  12.2 us (11%)
  waiting for transfers between devices  11.4 us (10%)
    all_to_all x1, blocking collectives, shards(): lax.all_to_all(operand, 'member', split_axis=0, concat_axis=0, tiled=True)  44.1 us
    all_to_all x1, blocking collectives, shards(): lax.all_to_all(total.reshape(chips, rows, own), 'member', split_axis=0, c...  21.6 us
    pallas_call x1, Pallas kernels, shards(): windowed(near_kernel, (total, half_own, half_own, tapers), [SMEM, VMEM, V...  14.3 us
    ppermute x1, waiting for transfers between devices, shards(): halo_weights = lax.ppermute(mine[:, rows:, :HALO * TILE], axes, out)  5.45 us
    ppermute x1, starting transfers between devices, shards(): lax.ppermute(jnp.where(upper, back[half:], back[:half]), 'region', swap)  4.9 us
    ppermute x1, starting transfers between devices, shards(): got = lax.ppermute(sent, 'region', swap)  3.32 us
    pallas_call x1, Pallas kernels, shards(): copying(send_kernel, jax.ShapeDtypeStruct((half, 2 * rows, own), F32), [S...  3.24 us
    pallas_call x1, Pallas kernels, shards(): windowed(far_kernel, (coefficient, coefficient), [VMEM] * 5, [(HALO * TIL...  2.44 us
  transfers between devices with their start and end apart: 7, of which 4 were waited for; matrix products, arithmetic and copies ran while one was open for 1% of the time, Pallas kernels for 15%

profile of v5, /device:TPU:1, one launch (start us, length us, event | category | flops | bytes accessed | tf_op | source)
XLA Modules:
  0.0 115.3 jit_solution(17889385767862901550)
XLA Ops:
  0.0 3.2 %send.1 = f32[8,32,1536]{2,1,0:T(8,128)} custom-call(s32[1]{0:T(128)} %bitcast.core_ref, f32[16,24576]{1,0:T(8,128)} %states_ref.1, f32[16,24576]{1,0:T(8,128)} %weights_ref.1), custom_call_target="tpu_custom_call" | custom-call | bytes 6000000 | tf_op jit(solution)/shard_map/send/pallas_call | solution.py:302
  3.3 3.3 %collective-permute-start.1 = (f32[8,32,1536]{2,1,0:T(8,128)}, f32[8,32,1536]{2,1,0:T(8,128)}, u32[]{:S(2)}, u32[]{:S(2)}) collective-permute-start(f32[8,32,1536]{2,1,0:T(8,128)} %send.1), channel_id=1, source_target_pairs={{0,1},{1,0},{2,3},{3,2},{4,5},{5,4},{6,7},{7,6},{8,9},{9,8},{10,11... | collective-permute-start | bytes 4718600 | tf_op jit(solution)/shard_map/ppermute | solution.py:311
  6.6 0.1 collective-permute-start.2
  6.7 0.4 collective-permute-start
  7.2 2.3 %collective-permute-done.2 = s32[192,12]{0,1:T(8,128)S(1)} collective-permute-done((s32[192,12]{0,1:T(8,128)S(1)}, s32[192,12]{0,1:T(8,128)S(1)}, u32[]{:S(2)}, u32[]{:S(2)}) %collective-permute-start.2) | collective-permute-done | bytes 9248 | tf_op jit(solution)/shard_map/ppermute | solution.py:257
  9.8 0.1 compare_reduce_fusion
  9.9 0.1 copy.8
  10.1 0.2 broadcast_in_dim.14
  10.4 1.7 %merge.1 = f32[16,32,1536]{2,1,0:T(8,128)S(1)} custom-call(s32[1]{0:T(128)} %bitcast.core_ref, s32[1]{0:T(128)} %bitcast.1.odd_ref, s32[192]{0:T(256)S(1)} %copy-done.2, s32[192]{0:T(256)S(1)} %collective-permute-done.theirs_ref, f32[16,24576]{1,0:T(8,128)S(1)} %copy-done, f32[16,24576]{1,0:T(8,128)S(1)} %copy-done.1, ...), custom_call_target="tpu_custom_call" | custom-call | bytes 6000000 | tf_op jit(solution)/shard_map/merge/pallas_call | solution.py:312
  12.0 44.1 %all_to_all.10.mine_ref = f32[16,32,1536]{2,1,0:T(8,128)S(1)} all-to-all(f32[16,32,1536]{2,1,0:T(8,128)S(1)} %merge.1), channel_id=1, replica_groups=mesh['member'=16,'region'=16] {'member'}, dimensions={0} | all-to-all | bytes 6291456 | tf_op jit(solution)/shard_map/all_to_all | solution.py:321
  56.1 0.1 slice.25
  56.2 1.7 %collective-permute-start.4 = (f32[16,32,1024]{2,1,0:T(8,128)S(1)}, f32[16,32,1024]{2,1,0:T(8,128)S(1)}, u32[]{:S(2)}, u32[]{:S(2)}) collective-permute-start(f32[16,32,1024]{2,1,0:T(8,128)S(1)} %slice.25), channel_id=1, source_target_pairs={{0,1},{1,0},{2,3},{3,2},{4,5},{5,4},{6,7},{7,6},{8,9},{9,8},{10,11... | collective-permute-start | bytes 6291464 | tf_op jit(solution)/shard_map/ppermute | solution.py:325
  57.9 0.2 fusion.3
  58.1 0.3 collective-permute-start.5
  58.4 1.6 %collective-permute-start.3 = (f32[16,16,1024]{2,1,0:T(8,128)S(1)}, f32[16,16,1024]{2,1,0:T(8,128)S(1)}, u32[]{:S(2)}, u32[]{:S(2)}) collective-permute-start(f32[16,16,1024]{2,1,0:T(8,128)S(1)} %get-tuple-element.30), channel_id=1, source_target_pairs={{0,15},{1,16},{16,1},{17,32},{32,17},{33,48},{48,33},{49,112},{112... | collective-permute-start | bytes 3145736 | tf_op jit(solution)/shard_map/ppermute | solution.py:324
  59.9 1.8 %collective-permute-done.4.other_ref = f32[16,32,1024]{2,1,0:T(8,128)S(1)} collective-permute-done((f32[16,32,1024]{2,1,0:T(8,128)S(1)}, f32[16,32,1024]{2,1,0:T(8,128)S(1)}, u32[]{:S(2)}, u32[]{:S(2)}) %collective-permute-start.4) | collective-permute-done | bytes 2097184 | tf_op jit(solution)/shard_map/ppermute | solution.py:325
  61.7 14.3 %near.1 = (f32[256,1536]{1,0:T(8,128)S(1)}, bf16[256,1536]{1,0:T(8,128)(2,1)S(1)}, bf16[256,1536]{1,0:T(8,128)(2,1)S(1)}, f32[2304,256]{1,0:T(8,128)S(1)}) custom-call(s32[1]{0:T(128)} %bitcast.core_ref, f32[108,256]{1,0:T(8,128)S(1)} %bitcast.10, f32[16,32,1536]{2,1,0:T(8,128)S(1)} %all_to_all.10.mine_ref, f32[16,32,1024]{2,1,0:T(8,128)S(1)} %collective-permute-done.4.other_ref), custom_call_target="tpu_custom_call" | custom-call | flops 17999998976 | bytes 8000000 | tf_op jit(solution)/shard_map/near/pallas_call | solution.py:330
  76.0 2.4 %far.1 = (bf16[4096,256]{1,0:T(8,128)(2,1)S(1)}, bf16[4096,256]{1,0:T(8,128)(2,1)S(1)}) custom-call(f32[108,256]{1,0:T(8,128)S(1)} %bitcast.11, f32[16,16,1024]{2,1,0:T(8,128)S(1)} %collective-permute-done.5.halo_ref, bf16[256,1536]{1,0:T(8,128)(2,1)S(1)} %get-tuple-element.23.ah, bf16[256,1536]{1,0:T(8,128)(2,1)S(1)} %get-tuple-element.24.al, ...), custom_call_target="tpu_custom_call" | custom-call | flops 2000000000 | bytes 8000000 | tf_op jit(solution)/shard_map/far/pallas_call | solution.py:339
  78.5 5.4 %collective-permute-done.3.halo_ref = f32[16,16,1024]{2,1,0:T(8,128)S(1)} collective-permute-done((f32[16,16,1024]{2,1,0:T(8,128)S(1)}, f32[16,16,1024]{2,1,0:T(8,128)S(1)}, u32[]{:S(2)}, u32[]{:S(2)}) %collective-permute-start.3) | collective-permute-done | bytes 1048608 | tf_op jit(solution)/shard_map/ppermute | solution.py:324
  83.9 1.6 %add.111 = f32[256,1536]{1,0:T(8,128)S(1)} custom-call(f32[16,16,1024]{2,1,0:T(8,128)S(1)} %collective-permute-done.3.halo_ref, f32[256,1536]{1,0:T(8,128)S(1)} %get-tuple-element.22.near_ref, bf16[4096,256]{1,0:T(8,128)(2,1)S(1)} %get-tuple-element.26.ch, bf16[4096,256]{1,0:T(8,128)(2,1)S(1)} %get-tuple-element.27.cl), custom_call_target="tpu_custom_call" | custom-call | flops 2000000000 | bytes 8000000 | tf_op jit(solution)/shard_map/add/pallas_call | solution.py:347
  85.5 21.6 %all_to_all.11.back_ref = f32[16,16,1536]{2,1,0:T(8,128)S(1)} all-to-all(f32[16,16,1536]{2,1,0:T(8,128)S(1)} %bitcast.9), channel_id=1, replica_groups=mesh['member'=16,'region'=16] {'member'}, dimensions={0} | all-to-all | bytes 3145728 | tf_op jit(solution)/shard_map/all_to_all | solution.py:350
  107.2 4.9 %collective-permute-start.6 = (f32[8,16,1536]{2,1,0:T(8,128)S(1)}, f32[8,16,1536]{2,1,0:T(8,128)S(1)}, u32[]{:S(2)}, u32[]{:S(2)}) collective-permute-start(f32[8,16,1536]{2,1,0:T(8,128)S(1)} %slice_select_fusion), channel_id=1, source_target_pairs={{0,1},{1,0},{2,3},{3,2},{4,5},{5,4},{6,7},{7,6},{8,9},{9,8},{10,11... | collective-permute-start | bytes 2359304 | tf_op jit(solution)/shard_map/ppermute | solution.py:351
  112.1 1.9 %collective-permute-done.6.got_ref = f32[8,16,1536]{2,1,0:T(8,128)S(1)} collective-permute-done((f32[8,16,1536]{2,1,0:T(8,128)S(1)}, f32[8,16,1536]{2,1,0:T(8,128)S(1)}, u32[]{:S(2)}, u32[]{:S(2)}) %collective-permute-start.6) | collective-permute-done | bytes 786464 | tf_op jit(solution)/shard_map/ppermute | solution.py:351
  114.0 1.2 %place.1 = f32[16,24576]{1,0:T(8,128)} custom-call(s32[1]{0:T(128)} %bitcast.core_ref, s32[1]{0:T(128)} %bitcast.1.odd_ref, f32[16,16,1536]{2,1,0:T(8,128)S(1)} %all_to_all.11.back_ref, f32[8,16,1536]{2,1,0:T(8,128)S(1)} %collective-permute-done.6.got_ref), custom_call_target="tpu_custom_call" | custom-call | bytes 6000000 | tf_op jit(solution)/shard_map/place/pallas_call | solution.py:352
  (23 shorter events, 0.5 us)
Async XLA Ops:
  0.0 6.6 %copy-start.3 = (s32[192,12]{0,1:T(8,128)S(1)}, s32[192,12]{0,1:T(8,128)}, u32[]{:S(2)}) copy-start(s32[192,12]{0,1:T(8,128)} %param.7) | copy-start | bytes 27652
  0.0 6.7 %copy-start.2 = (s32[192]{0:T(256)S(1)}, s32[192]{0:T(256)}, u32[]{:S(2)}) copy-start(s32[192]{0:T(256)} %counts_ref) | copy-start | bytes 2308
  0.0 10.3 %copy-start = (f32[16,24576]{1,0:T(8,128)S(1)}, f32[16,24576]{1,0:T(8,128)}, u32[]{:S(2)}) copy-start(f32[16,24576]{1,0:T(8,128)} %states_ref.1) | copy-start | bytes 4718596
  0.0 10.3 %copy-start.1 = (f32[16,24576]{1,0:T(8,128)S(1)}, f32[16,24576]{1,0:T(8,128)}, u32[]{:S(2)}) copy-start(f32[16,24576]{1,0:T(8,128)} %weights_ref.1) | copy-start | bytes 4718596
  3.3 7.1 %collective-permute-start.1 = (f32[8,32,1536]{2,1,0:T(8,128)}, f32[8,32,1536]{2,1,0:T(8,128)}, u32[]{:S(2)}, u32[]{:S(2)}) collective-permute-start(f32[8,32,1536]{2,1,0:T(8,128)} %send.1), channel_id=1, source_target_pairs={{0,1},{1,0},{2,3},{3,2},{4,5},{5,4},{6,7},{7,6},{8,9},{9,8},{10,11... | collective-permute-start | bytes 4718600 | tf_op jit(solution)/shard_map/ppermute | solution.py:311
  6.6 2.9 %collective-permute-start.2 = (s32[192,12]{0,1:T(8,128)S(1)}, s32[192,12]{0,1:T(8,128)S(1)}, u32[]{:S(2)}, u32[]{:S(2)}) collective-permute-start(s32[192,12]{0,1:T(8,128)S(1)} %copy-done.3), channel_id=1, source_target_pairs={{0,1},{1,0},{2,3},{3,2},{4,5},{5,4},{6,7},{7,6},{8,9},{9,8},{10,11... | collective-permute-start | bytes 27656 | tf_op jit(solution)/shard_map/ppermute | solution.py:257
  6.7 3.6 %collective-permute-start = (s32[192]{0:T(256)S(1)}, s32[192]{0:T(256)S(1)}, u32[]{:S(2)}, u32[]{:S(2)}) collective-permute-start(s32[192]{0:T(256)S(1)} %copy-done.2), channel_id=1, source_target_pairs={{0,1},{1,0},{2,3},{3,2},{4,5},{5,4},{6,7},{7,6},{8,9},{9,8},{10,11... | collective-permute-start | bytes 2312 | tf_op jit(solution)/shard_map/ppermute | solution.py:317
  56.2 5.4 %collective-permute-start.4 = (f32[16,32,1024]{2,1,0:T(8,128)S(1)}, f32[16,32,1024]{2,1,0:T(8,128)S(1)}, u32[]{:S(2)}, u32[]{:S(2)}) collective-permute-start(f32[16,32,1024]{2,1,0:T(8,128)S(1)} %slice.25), channel_id=1, source_target_pairs={{0,1},{1,0},{2,3},{3,2},{4,5},{5,4},{6,7},{7,6},{8,9},{9,8},{10,11... | collective-permute-start | bytes 6291464 | tf_op jit(solution)/shard_map/ppermute | solution.py:325
  58.1 17.9 %collective-permute-start.5 = (f32[16,16,1024]{2,1,0:T(8,128)S(1)}, f32[16,16,1024]{2,1,0:T(8,128)S(1)}, u32[]{:S(2)}, u32[]{:S(2)}) collective-permute-start(f32[16,16,1024]{2,1,0:T(8,128)S(1)} %get-tuple-element.29), channel_id=1, source_target_pairs={{0,15},{1,16},{16,1},{17,32},{32,17},{33,48},{48,33},{49,112},{112... | collective-permute-start | bytes 3145736 | tf_op jit(solution)/shard_map/ppermute | solution.py:323
  58.4 25.6 %collective-permute-start.3 = (f32[16,16,1024]{2,1,0:T(8,128)S(1)}, f32[16,16,1024]{2,1,0:T(8,128)S(1)}, u32[]{:S(2)}, u32[]{:S(2)}) collective-permute-start(f32[16,16,1024]{2,1,0:T(8,128)S(1)} %get-tuple-element.30), channel_id=1, source_target_pairs={{0,15},{1,16},{16,1},{17,32},{32,17},{33,48},{48,33},{49,112},{112... | collective-permute-start | bytes 3145736 | tf_op jit(solution)/shard_map/ppermute | solution.py:324
  107.2 6.8 %collective-permute-start.6 = (f32[8,16,1536]{2,1,0:T(8,128)S(1)}, f32[8,16,1536]{2,1,0:T(8,128)S(1)}, u32[]{:S(2)}, u32[]{:S(2)}) collective-permute-start(f32[8,16,1536]{2,1,0:T(8,128)S(1)} %slice_select_fusion), channel_id=1, source_target_pairs={{0,1},{1,0},{2,3},{3,2},{4,5},{5,4},{6,7},{7,6},{8,9},{9,8},{10,11... | collective-permute-start | bytes 2359304 | tf_op jit(solution)/shard_map/ppermute | solution.py:351
